TPU v7x, 32 devices: a whole 2x2x4 slice. The times are simulated.
32 devices in a mesh: dp: 32 (over z, y, x, core).
Axes of the slice: x: 2, y: 2, z: 4, core: 2. Of those that a mesh axis runs over, the one named last changes fastest.
Arguments:
- hidden: bfloat16 [14592, 768], P('dp'), may hold values from -6 to 6
- region_count: int32 [64], P('dp'), may hold values from 10 to 100
- text_mask: int32 [64, 128], P('dp'), may hold values 0 or 1
- q_weight: bfloat16 [2, 768, 768], P(None, 'dp'), may hold values from -0.21875 to 0.21875
- k_weight: bfloat16 [2, 768, 768], P(None, 'dp'), may hold values from -0.21875 to 0.21875
- v_weight: bfloat16 [2, 768, 768], P(None, 'dp'), may hold values from -0.21875 to 0.21875
- o_weight: bfloat16 [2, 768, 768], P(None, 'dp'), may hold values from -0.75 to 0.75
- q_bias: bfloat16 [2, 768], P(None, 'dp'), may hold values from -3 to 3
- v_bias: bfloat16 [2, 768], P(None, 'dp'), may hold values from -3 to 3
- o_bias: bfloat16 [2, 768], P(None, 'dp'), may hold values from -3 to 3
- gain_one: bfloat16 [2, 768], P(None, 'dp'), may hold values from 0.099609375 to 1.8984375
- shift_one: bfloat16 [2, 768], P(None, 'dp'), may hold values from -3 to 3
- up_weight: bfloat16 [2, 768, 3072], P(None, 'dp'), may hold values from -0.21875 to 0.21875
- up_bias: bfloat16 [2, 3072], P(None, 'dp'), may hold values from -3 to 3
- down_weight: bfloat16 [2, 3072, 768], P(None, 'dp'), may hold values from -0.109375 to 0.109375
- down_bias: bfloat16 [2, 768], P(None, 'dp'), may hold values from -3 to 3
- gain_two: bfloat16 [2, 768], P(None, 'dp'), may hold values from 0.099609375 to 1.8984375
- shift_two: bfloat16 [2, 768], P(None, 'dp'), may hold values from -3 to 3
- cotangent: bfloat16 [14592, 768], P('dp'), may hold values from -6 to 6
Outputs:
- layer_output: bfloat16 [14592, 768], P('dp')
- hidden_grad: float32 [14592, 768], P('dp')
- q_weight_grad: float32 [2, 768, 768], P(None, 'dp')
- k_weight_grad: float32 [2, 768, 768], P(None, 'dp')
- v_weight_grad: float32 [2, 768, 768], P(None, 'dp')
- o_weight_grad: float32 [2, 768, 768], P(None, 'dp')
- q_bias_grad: float32 [2, 768], P(None, 'dp')
- v_bias_grad: float32 [2, 768], P(None, 'dp')
- o_bias_grad: float32 [2, 768], P(None, 'dp')
- gain_one_grad: float32 [2, 768], P(None, 'dp')
- shift_one_grad: float32 [2, 768], P(None, 'dp')
- up_weight_grad: float32 [2, 768, 3072], P(None, 'dp')
- up_bias_grad: float32 [2, 3072], P(None, 'dp')
- down_weight_grad: float32 [2, 3072, 768], P(None, 'dp')
- down_bias_grad: float32 [2, 768], P(None, 'dp')
- gain_two_grad: float32 [2, 768], P(None, 'dp')
- shift_two_grad: float32 [2, 768], P(None, 'dp')
Inputs may be any that keep to these rules, and one draw needn't show every extreme that they name: `region_count`: region slots at or after an item's count are masked as keys.
All inputs are finite; a program needn't handle non-finite values. No bound on the sum of `text_mask` on one device may be relied on, other than what follows from the above.
Results may differ from a plain program's by a relative error of at most 0.03.
Values may be sent and summed in bfloat16 or wider, within the bound.
No kernel may reach another device: no remote copies, remote signals or barrier semaphores. Data moves between devices by JAX's collectives and lax.ppermute only.
A program may use at most 256 MiB of HBM per device.

v0:
```python
import jax
import jax.numpy as jnp
from jax import lax
from jax.sharding import PartitionSpec as P

HEADS = 12
HEAD_DIM = 64
REGIONS = 100


epsilon = 1e-12


def layer_norm(values, gain, shift):
    center = values - jnp.mean(values, axis=-1, keepdims=True)
    spread = jnp.mean(center * center, axis=-1, keepdims=True)
    return center * lax.rsqrt(spread + epsilon) * gain + shift


def exact_gelu(values):
    return jax.nn.gelu(values, approximate=False)


def row_softmax(values):
    return jax.nn.softmax(values, axis=-1)


def dense(left, right):
    return jnp.dot(left, right, preferred_element_type=jnp.float32)


def outer(left, right):
    return lax.dot_general(
        left, right, (((0,), (0,)), ((), ())), preferred_element_type=jnp.float32
    )


def back_dense(left, right):
    return lax.dot_general(
        left, right, (((1,), (1,)), ((), ())), preferred_element_type=jnp.float32
    )


def column_sum(values):
    return jnp.sum(values.astype(jnp.float32), axis=0)


def slot_valid(region_count, text_mask):
    region_slot = jnp.arange(REGIONS, dtype=jnp.int32)[None, :] < region_count[:, None]
    return jnp.concatenate([text_mask.astype(jnp.float32), region_slot.astype(jnp.float32)], axis=1)


def fetch_forward(stacked, layer_index):
    shard = tuple((weight[layer_index] for weight in stacked))
    return (
        lax.all_gather(shard[0], "dp", axis=0, tiled=True),
        lax.all_gather(shard[1], "dp", axis=0, tiled=True),
        lax.all_gather(shard[2], "dp", axis=0, tiled=True),
        lax.all_gather(shard[3], "dp", axis=0, tiled=True),
        lax.all_gather(shard[4], "dp", axis=0, tiled=True),
        lax.all_gather(shard[5], "dp", axis=0, tiled=True),
        lax.all_gather(shard[6], "dp", axis=0, tiled=True),
        lax.all_gather(shard[7], "dp", axis=0, tiled=True),
        lax.all_gather(shard[8], "dp", axis=0, tiled=True),
        lax.all_gather(shard[9], "dp", axis=0, tiled=True),
        lax.all_gather(shard[10], "dp", axis=0, tiled=True),
        lax.all_gather(shard[11], "dp", axis=0, tiled=True),
        lax.all_gather(shard[12], "dp", axis=0, tiled=True),
        lax.all_gather(shard[13], "dp", axis=0, tiled=True),
        lax.all_gather(shard[14], "dp", axis=0, tiled=True),
    )


def fetch_backward(stacked, layer_index):
    shard = tuple((weight[layer_index] for weight in stacked))
    return (
        lax.all_gather(shard[0], "dp", axis=0, tiled=True),
        lax.all_gather(shard[1], "dp", axis=0, tiled=True),
        lax.all_gather(shard[2], "dp", axis=0, tiled=True),
        lax.all_gather(shard[3], "dp", axis=0, tiled=True),
        lax.all_gather(shard[4], "dp", axis=0, tiled=True),
        lax.all_gather(shard[5], "dp", axis=0, tiled=True),
        lax.all_gather(shard[6], "dp", axis=0, tiled=True),
        lax.all_gather(shard[7], "dp", axis=0, tiled=True),
        lax.all_gather(shard[8], "dp", axis=0, tiled=True),
        lax.all_gather(shard[9], "dp", axis=0, tiled=True),
        lax.all_gather(shard[10], "dp", axis=0, tiled=True),
        lax.all_gather(shard[11], "dp", axis=0, tiled=True),
        lax.all_gather(shard[12], "dp", axis=0, tiled=True),
        lax.all_gather(shard[13], "dp", axis=0, tiled=True),
        lax.all_gather(shard[14], "dp", axis=0, tiled=True),
    )


def pack_owned(grads, owners):
    return jnp.concatenate([member.reshape(owners, -1) for member in grads], axis=1)


def unpack_owned(flat_row, grads, owners):
    pieces = []
    offset = 0
    for member in grads:
        share = member.size // owners
        block_shape = (member.shape[0] // owners,) + tuple(member.shape[1:])
        pieces.append(flat_row[offset : offset + share].reshape(block_shape))
        offset = offset + share
    return tuple(pieces)


def reduce_each(grads):
    owners = lax.axis_size("dp")
    summed = lax.psum_scatter(pack_owned(grads, owners), "dp", scatter_dimension=0, tiled=True)
    return unpack_owned(summed[0], grads, owners)


def recompute(inputs, gathered, valid_keys):
    (
        q_weight,
        k_weight,
        v_weight,
        o_weight,
        q_bias,
        v_bias,
        o_bias,
        gain_one,
        shift_one,
        up_weight,
        up_bias,
        down_weight,
        down_bias,
        gain_two,
        shift_two,
    ) = gathered
    item_count = valid_keys.shape[0]
    row_count = inputs.shape[0]
    seq_length = row_count // item_count
    width = q_weight.shape[1]

    def heads_of(values):
        return values.reshape(item_count, seq_length, HEADS, HEAD_DIM)

    queries = (dense(inputs, q_weight) + q_bias.astype(jnp.float32)).astype(jnp.bfloat16)
    key_rows = dense(inputs, k_weight).astype(jnp.bfloat16)
    value_rows = (dense(inputs, v_weight) + v_bias.astype(jnp.float32)).astype(jnp.bfloat16)
    scores = (
        jnp.einsum(
            "bqhd,bkhd->bhqk",
            heads_of(queries),
            heads_of(key_rows),
            preferred_element_type=jnp.float32,
        )
        * 0.125
    )
    scores = scores + (valid_keys[:, None, None, :] - 1.0) * 10000.0
    attention_low = row_softmax(scores).astype(jnp.bfloat16)
    context = jnp.einsum(
        "bhqk,bkhd->bqhd", attention_low, heads_of(value_rows), preferred_element_type=jnp.float32
    )
    context = context.astype(jnp.bfloat16).reshape(row_count, width)
    attended = dense(context, o_weight) + o_bias.astype(jnp.float32)
    first_sum = inputs.astype(jnp.float32) + attended
    middle = layer_norm(
        first_sum, gain_one.astype(jnp.float32), shift_one.astype(jnp.float32)
    ).astype(jnp.bfloat16)
    lifted = dense(middle, up_weight) + up_bias.astype(jnp.float32)
    activated = exact_gelu(lifted).astype(jnp.bfloat16)
    lowered = dense(activated, down_weight) + down_bias.astype(jnp.float32)
    second_sum = middle.astype(jnp.float32) + lowered
    output = layer_norm(
        second_sum, gain_two.astype(jnp.float32), shift_two.astype(jnp.float32)
    ).astype(jnp.bfloat16)
    return (
        output,
        (
            queries,
            key_rows,
            value_rows,
            scores,
            attention_low,
            context,
            first_sum,
            middle,
            lifted,
            activated,
            second_sum,
        ),
    )


def backward(inputs, gathered, saved, out_grad):
    (
        q_weight,
        k_weight,
        v_weight,
        o_weight,
        q_bias,
        v_bias,
        o_bias,
        gain_one,
        shift_one,
        up_weight,
        up_bias,
        down_weight,
        down_bias,
        gain_two,
        shift_two,
    ) = gathered
    (
        queries,
        key_rows,
        value_rows,
        scores,
        attention_low,
        context,
        first_sum,
        middle,
        lifted,
        activated,
        second_sum,
    ) = saved
    item_count = attention_low.shape[0]
    seq_length = attention_low.shape[2]
    row_count = inputs.shape[0]
    width = q_weight.shape[1]

    def heads_of(values):
        return values.reshape(item_count, seq_length, HEADS, HEAD_DIM)

    unused, norm_pull = jax.vjp(
        layer_norm, second_sum, gain_two.astype(jnp.float32), shift_two.astype(jnp.float32)
    )
    sum_grad, gain_two_grad, shift_two_grad = norm_pull(out_grad)
    lowered_grad = sum_grad.astype(jnp.bfloat16)
    down_weight_grad = outer(activated, lowered_grad)
    down_bias_grad = column_sum(lowered_grad)
    activated_grad = back_dense(lowered_grad, down_weight)
    unused, gelu_pull = jax.vjp(exact_gelu, lifted)
    lifted_grad = gelu_pull(activated_grad)[0].astype(jnp.bfloat16)
    up_weight_grad = outer(middle, lifted_grad)
    up_bias_grad = column_sum(lifted_grad)
    middle_grad = sum_grad + back_dense(lifted_grad, up_weight)
    unused, first_pull = jax.vjp(
        layer_norm, first_sum, gain_one.astype(jnp.float32), shift_one.astype(jnp.float32)
    )
    first_grad, gain_one_grad, shift_one_grad = first_pull(middle_grad)
    attended_grad = first_grad.astype(jnp.bfloat16)
    o_weight_grad = outer(context, attended_grad)
    o_bias_grad = column_sum(attended_grad)
    context_grad = heads_of(back_dense(attended_grad, o_weight).astype(jnp.bfloat16))
    attention_grad = jnp.einsum(
        "bqhd,bkhd->bhqk", context_grad, heads_of(value_rows), preferred_element_type=jnp.float32
    )
    value_grad = jnp.einsum(
        "bhqk,bqhd->bkhd", attention_low, context_grad, preferred_element_type=jnp.float32
    )
    value_grad = value_grad.astype(jnp.bfloat16).reshape(row_count, width)
    unused, soft_pull = jax.vjp(row_softmax, scores)
    score_grad = soft_pull(attention_grad)[0].astype(jnp.bfloat16)
    query_grad = (
        jnp.einsum(
            "bhqk,bkhd->bqhd", score_grad, heads_of(key_rows), preferred_element_type=jnp.float32
        )
        * 0.125
    )
    query_grad = query_grad.astype(jnp.bfloat16).reshape(row_count, width)
    key_grad = (
        jnp.einsum(
            "bhqk,bqhd->bkhd", score_grad, heads_of(queries), preferred_element_type=jnp.float32
        )
        * 0.125
    )
    key_grad = key_grad.astype(jnp.bfloat16).reshape(row_count, width)
    q_weight_grad = outer(inputs, query_grad)
    k_weight_grad = outer(inputs, key_grad)
    v_weight_grad = outer(inputs, value_grad)
    q_bias_grad = column_sum(query_grad)
    v_bias_grad = column_sum(value_grad)
    input_grad = (
        first_grad
        + back_dense(query_grad, q_weight)
        + back_dense(key_grad, k_weight)
        + back_dense(value_grad, v_weight)
    )
    gradients = (
        q_weight_grad,
        k_weight_grad,
        v_weight_grad,
        o_weight_grad,
        q_bias_grad,
        v_bias_grad,
        o_bias_grad,
        gain_one_grad,
        shift_one_grad,
        up_weight_grad,
        up_bias_grad,
        down_weight_grad,
        down_bias_grad,
        gain_two_grad,
        shift_two_grad,
    )
    return (gradients, input_grad)


def shards(
    hidden,
    region_count,
    text_mask,
    q_weight,
    k_weight,
    v_weight,
    o_weight,
    q_bias,
    v_bias,
    o_bias,
    gain_one,
    shift_one,
    up_weight,
    up_bias,
    down_weight,
    down_bias,
    gain_two,
    shift_two,
    cotangent,
):
    valid_keys = slot_valid(region_count, text_mask)
    stacked = (
        q_weight,
        k_weight,
        v_weight,
        o_weight,
        q_bias,
        v_bias,
        o_bias,
        gain_one,
        shift_one,
        up_weight,
        up_bias,
        down_weight,
        down_bias,
        gain_two,
        shift_two,
    )
    layer_count = q_weight.shape[0]
    saved_inputs = [hidden]
    current = hidden
    kept_weights = None
    kept_layers = []
    for layer_index in range(layer_count):
        kept_weights = fetch_forward(stacked, layer_index)
        kept_layers.append(kept_weights)
        current, unused = recompute(current, kept_weights, valid_keys)
        saved_inputs.append(current)
    flowing = cotangent.astype(jnp.float32)
    per_layer = [None] * layer_count
    for layer_index in reversed(range(layer_count)):
        gathered = fetch_backward(stacked, layer_index)
        layer_input = saved_inputs[layer_index]
        unused, saved = recompute(layer_input, gathered, valid_keys)
        gradients, flowing = backward(layer_input, gathered, saved, flowing)
        gradients = reduce_each(gradients)
        per_layer[layer_index] = gradients
    outputs = tuple(
        (
            jnp.stack([per_layer[layer_index][member_index] for layer_index in range(layer_count)])
            for member_index in range(15)
        )
    )
    return (
        saved_inputs[-1],
        flowing,
        outputs[0],
        outputs[1],
        outputs[2],
        outputs[3],
        outputs[4],
        outputs[5],
        outputs[6],
        outputs[7],
        outputs[8],
        outputs[9],
        outputs[10],
        outputs[11],
        outputs[12],
        outputs[13],
        outputs[14],
    )


def solution(mesh):
    return jax.shard_map(
        shards,
        mesh=mesh,
        in_specs=(
            P("dp", None),
            P("dp"),
            P("dp", None),
            P(None, "dp", None),
            P(None, "dp", None),
            P(None, "dp", None),
            P(None, "dp", None),
            P(None, "dp"),
            P(None, "dp"),
            P(None, "dp"),
            P(None, "dp"),
            P(None, "dp"),
            P(None, "dp", None),
            P(None, "dp"),
            P(None, "dp", None),
            P(None, "dp"),
            P(None, "dp"),
            P(None, "dp"),
            P("dp", None),
        ),
        out_specs=(
            P("dp", None),
            P("dp", None),
            P(None, "dp", None),
            P(None, "dp", None),
            P(None, "dp", None),
            P(None, "dp", None),
            P(None, "dp"),
            P(None, "dp"),
            P(None, "dp"),
            P(None, "dp"),
            P(None, "dp"),
            P(None, "dp", None),
            P(None, "dp"),
            P(None, "dp", None),
            P(None, "dp"),
            P(None, "dp"),
            P(None, "dp"),
        ),
        check_vma=False,
    )
```

profile of v0, /device:TPU:0, one launch (start us, length us, event | category | flops | bytes accessed | tf_op | source)
XLA Modules:
  0.0 1934.7 jit_solution(17813821299577899693)
XLA Ops:
  31.4 43.3 %all-reduce.21 = (bf16[768]{0:T(1024)(128)(2,1)S(1)}, bf16[768]{0:T(1024)(128)(2,1)S(1)}, bf16[768]{0:T(1024)(128)(2,1)S(1)}, bf16[768]{0:T(1024)(128)(2,1)S(1)}...) all-reduce(bf16[768]{0:T(1024)(128)(2,1)S(1)} %dynamic-update-slice, ...), channel_id=5, replica_groups=mesh['dp'=32] {'dp'}, use_global_device_ids=true, to_apply=%add.1 | all-reduce | flops 18432 | bytes 73728
  87.0 37.9 %all-gather.45.cloned.1.call-done = bf16[1,768,768]{2,1,0:T(8,128)(2,1)} async-done(((bf16[1,24,768]{2,1,0:T(8,128)(2,1)}), bf16[1,768,768]{2,1,0:T(8,128)(2,1)}) %all-gather.45.cloned.1.call-update) | async-done | bytes 1179664 | tf_op jit(solution)/shard_map/all_gather | solution.py:56
  136.1 45.3 %all-gather.43.cloned.1.call-done = bf16[1,768,768]{2,1,0:T(8,128)(2,1)} async-done(((bf16[1,24,768]{2,1,0:T(8,128)(2,1)}), bf16[1,768,768]{2,1,0:T(8,128)(2,1)}) %all-gather.43.cloned.1.call-update) | async-done | bytes 1179664 | tf_op jit(solution)/shard_map/all_gather | solution.py:58
  192.9 44.2 %all-gather.49.cloned.1.call-done = bf16[1,768,768]{2,1,0:T(8,128)(2,1)} async-done(((bf16[1,24,768]{2,1,0:T(8,128)(2,1)}), bf16[1,768,768]{2,1,0:T(8,128)(2,1)}) %all-gather.49.cloned.1.call-update) | async-done | bytes 1179664 | tf_op jit(solution)/shard_map/all_gather | solution.py:59
  239.6 63.4 %all-gather.51.cloned.1.call-done = bf16[1,768,3072]{2,1,0:T(8,128)(2,1)} async-done(((bf16[1,24,3072]{2,1,0:T(8,128)(2,1)}), bf16[1,768,3072]{2,1,0:T(8,128)(2,1)}) %all-gather.51.cloned.1.call-update) | async-done | bytes 4718608 | tf_op jit(solution)/shard_map/all_gather | solution.py:65
  303.1 18.3 multiply_convert_fusion.3
  321.4 47.5 %all-gather.53.cloned.1.call-done = bf16[1,3072,768]{2,1,0:T(8,128)(2,1)} async-done(((bf16[1,96,768]{2,1,0:T(8,128)(2,1)}), bf16[1,3072,768]{2,1,0:T(8,128)(2,1)}) %all-gather.53.cloned.1.call-update) | async-done | bytes 4718608 | tf_op jit(solution)/shard_map/all_gather | solution.py:67
  368.9 5.7 fusion.155
  375.2 50.0 %all-gather.59.cloned.1.call-done = bf16[1,768,768]{2,1,0:T(8,128)(2,1)} async-done(((bf16[1,24,768]{2,1,0:T(8,128)(2,1)}), bf16[1,768,768]{2,1,0:T(8,128)(2,1)}) %all-gather.59.cloned.1.call-update) | async-done | bytes 1179664 | tf_op jit(solution)/shard_map/all_gather | solution.py:57
  430.8 50.3 %all-gather.57.cloned.1.call-done = bf16[1,768,768]{2,1,0:T(8,128)(2,1)} async-done(((bf16[1,24,768]{2,1,0:T(8,128)(2,1)}), bf16[1,768,768]{2,1,0:T(8,128)(2,1)}) %all-gather.57.cloned.1.call-update) | async-done | bytes 1179664 | tf_op jit(solution)/shard_map/all_gather | solution.py:56
  486.7 50.3 %all-gather.55.cloned.1.call-done = bf16[1,768,768]{2,1,0:T(8,128)(2,1)} async-done(((bf16[1,24,768]{2,1,0:T(8,128)(2,1)}), bf16[1,768,768]{2,1,0:T(8,128)(2,1)}) %all-gather.55.cloned.1.call-update) | async-done | bytes 1179664 | tf_op jit(solution)/shard_map/all_gather | solution.py:58
  543.4 6.3 fusion.156
  557.2 35.6 %all-gather.61.cloned.1.call-done = bf16[1,768,768]{2,1,0:T(8,128)(2,1)} async-done(((bf16[1,24,768]{2,1,0:T(8,128)(2,1)}), bf16[1,768,768]{2,1,0:T(8,128)(2,1)}) %all-gather.61.cloned.1.call-update) | async-done | bytes 1179664 | tf_op jit(solution)/shard_map/all_gather | solution.py:59
  596.6 62.3 %all-gather.63.cloned.1.call-done = bf16[1,768,3072]{2,1,0:T(8,128)(2,1)} async-done(((bf16[1,24,3072]{2,1,0:T(8,128)(2,1)}), bf16[1,768,3072]{2,1,0:T(8,128)(2,1)}) %all-gather.63.cloned.1.call-update) | async-done | bytes 4718608 | tf_op jit(solution)/shard_map/all_gather | solution.py:65
  658.9 18.6 multiply_convert_fusion.2
  677.5 47.2 %all-gather.65.cloned.1.call-done = bf16[1,3072,768]{2,1,0:T(8,128)(2,1)} async-done(((bf16[1,96,768]{2,1,0:T(8,128)(2,1)}), bf16[1,3072,768]{2,1,0:T(8,128)(2,1)}) %all-gather.65.cloned.1.call-update) | async-done | bytes 4718608 | tf_op jit(solution)/shard_map/all_gather | solution.py:67
  724.7 5.7 fusion.166
  733.2 7.5 convert_reduce_fusion
  784.0 7.6 convert_reduce_fusion.1
  821.9 5.4 fusion.168
  834.7 5.4 fusion.167
  840.1 5.3 fusion.170
  874.1 8.1 reshape.487
  882.2 8.2 reshape.489
  924.2 8.1 reshape.472
  932.3 8.1 reshape.474
  970.6 28.8 %dynamic-update-slice.27 = f32[32,221472]{1,0:T(8,128)} dynamic-update-slice(f32[32,221472]{1,0:T(8,128)} %dynamic-update-slice.26, f32[32,73728]{1,0:T(8,128)} %reshape.487, s32[]{} %constant.231, s32[]{} %constant.240) | dynamic-update-slice | bytes 18874372
  999.3 28.8 %dynamic-update-slice.42 = f32[32,221472]{1,0:T(8,128)} dynamic-update-slice(f32[32,221472]{1,0:T(8,128)} %dynamic-update-slice.41, f32[32,73728]{1,0:T(8,128)} %reshape.472, s32[]{} %constant.231, s32[]{} %constant.240) | dynamic-update-slice | bytes 18874372
  1031.1 28.4 %dynamic-update-slice.29 = f32[32,221472]{1,0:T(8,128)} dynamic-update-slice(f32[32,221472]{1,0:T(8,128)} %dynamic-update-slice.28, f32[32,73728]{1,0:T(8,128)} %reshape.489, s32[]{} %constant.231, s32[]{} %constant.242) | dynamic-update-slice | bytes 18874372
  1059.5 28.4 %dynamic-update-slice.44 = f32[32,221472]{1,0:T(8,128)} dynamic-update-slice(f32[32,221472]{1,0:T(8,128)} %dynamic-update-slice.43, f32[32,73728]{1,0:T(8,128)} %reshape.474, s32[]{} %constant.231, s32[]{} %constant.242) | dynamic-update-slice | bytes 18874372
  1103.6 800.5 %all-reduce.24.cloned.1.call-done = (f32[32,221472]{1,0:T(8,128)}, f32[32,221472]{1,0:T(8,128)}) async-done(((f32[32,221472]{1,0:T(8,128)}, f32[32,221472]{1,0:T(8,128)}), (f32[32,221472]{1,0:T(8,128)}, f32[32,221472]{1,0:T(8,128)})) %all-reduce.24.cloned.1.call-update) | async-done | bytes 56696848
  1909.9 7.2 dynamic-slice_reduce_fusion
  (492 shorter events, 301.5 us)
Async XLA Ops:
  7.2 69.2 %copy-start.80 = (s32[2]{0:T(128)S(1)}, s32[2]{0:T(128)}, u32[]{:S(2)}) copy-start(s32[2]{0:T(128)} %param.20) | copy-start | bytes 28
  7.2 69.3 %copy-start.76 = (s32[2,128]{1,0:T(2,128)S(1)}, s32[2,128]{1,0:T(2,128)}, u32[]{:S(2)}) copy-start(s32[2,128]{1,0:T(2,128)} %param.21) | copy-start | bytes 3076
  7.2 77.0 %copy-start.22 = (bf16[456,768]{1,0:T(8,128)(2,1)S(1)}, bf16[456,768]{1,0:T(8,128)(2,1)}, u32[]{:S(2)}) copy-start(bf16[456,768]{1,0:T(8,128)(2,1)} %param.19) | copy-start | bytes 2101252
  7.2 77.0 %all-gather.47.cloned.1.call-start = ((), (), s32[]{:S(2)}) async-start(), calls=%async_computation.2 | async-start | bytes 1216512 | tf_op jit(solution)/shard_map/all_gather | solution.py:57
  8.8 116.1 %all-gather.45.cloned.1.call-start = ((), (), s32[]{:S(2)}) async-start(), calls=%async_computation.1 | async-start | bytes 1216512 | tf_op jit(solution)/shard_map/all_gather | solution.py:56
  10.3 171.1 %all-gather.43.cloned.1.call-start = ((), (), s32[]{:S(2)}) async-start(), calls=%async_computation | async-start | bytes 1216512 | tf_op jit(solution)/shard_map/all_gather | solution.py:58
  11.8 225.4 %all-gather.49.cloned.1.call-start = ((), (), s32[]{:S(2)}) async-start(), calls=%async_computation.3 | async-start | bytes 1216512 | tf_op jit(solution)/shard_map/all_gather | solution.py:59
  13.3 289.8 %all-gather.51.cloned.1.call-start = ((), (), s32[]{:S(2)}) async-start(), calls=%async_computation.4 | async-start | bytes 4866048 | tf_op jit(solution)/shard_map/all_gather | solution.py:65
  15.0 353.8 %all-gather.53.cloned.1.call-start = ((), (), s32[]{:S(2)}) async-start(), calls=%async_computation.5 | async-start | bytes 4866048 | tf_op jit(solution)/shard_map/all_gather | solution.py:67
  16.8 408.4 %all-gather.59.cloned.1.call-start = ((), (), s32[]{:S(2)}) async-start(), calls=%async_computation.8 | async-start | bytes 1216512 | tf_op jit(solution)/shard_map/all_gather | solution.py:57
  17.6 463.5 %all-gather.57.cloned.1.call-start = ((), (), s32[]{:S(2)}) async-start(), calls=%async_computation.7 | async-start | bytes 1216512 | tf_op jit(solution)/shard_map/all_gather | solution.py:56
  18.3 518.7 %all-gather.55.cloned.1.call-start = ((), (), s32[]{:S(2)}) async-start(), calls=%async_computation.6 | async-start | bytes 1216512 | tf_op jit(solution)/shard_map/all_gather | solution.py:58
  19.1 573.7 %all-gather.61.cloned.1.call-start = ((), (), s32[]{:S(2)}) async-start(), calls=%async_computation.9 | async-start | bytes 1216512 | tf_op jit(solution)/shard_map/all_gather | solution.py:59
  19.7 639.2 %all-gather.63.cloned.1.call-start = ((), (), s32[]{:S(2)}) async-start(), calls=%async_computation.10 | async-start | bytes 4866048 | tf_op jit(solution)/shard_map/all_gather | solution.py:65
  20.4 704.3 %all-gather.65.cloned.1.call-start = ((), (), s32[]{:S(2)}) async-start(), calls=%async_computation.11 | async-start | bytes 4866048 | tf_op jit(solution)/shard_map/all_gather | solution.py:67
  21.0 1883.1 %all-reduce.24.cloned.1.call-start = ((), (), s32[]{:S(2)}) async-start(), calls=%async_computation.12 | async-start | bytes 113442816
  192.9 110.1 %copy-start.57 = (f32[768]{0:T(1024)S(1)}, f32[768]{0:T(1024)}, u32[]{:S(2)}) copy-start(f32[768]{0:T(1024)} %convert_element_type.363) | copy-start | bytes 9220
  192.9 110.1 %copy-start.62 = (f32[3072]{0:T(1024)S(1)}, f32[3072]{0:T(1024)}, u32[]{:S(2)}) copy-start(f32[3072]{0:T(1024)} %convert_element_type.365) | copy-start | bytes 36868
  192.9 110.1 %copy-start.65 = (f32[768]{0:T(1024)S(1)}, f32[768]{0:T(1024)}, u32[]{:S(2)}) copy-start(f32[768]{0:T(1024)} %convert_element_type.364) | copy-start | bytes 9220
  239.3 129.6 %copy-start.24 = (f32[456,768]{1,0:T(8,128)}, f32[456,768]{1,0:T(8,128)S(1)}, u32[]{:S(2)}) copy-start(f32[456,768]{1,0:T(8,128)S(1)} %get-tuple-element.131) | copy-start | bytes 4202500
  239.6 81.8 %copy-start.55 = (f32[456]{0:T(512)}, f32[456]{0:T(512)S(1)}, u32[]{:S(2)}) copy-start(f32[456]{0:T(512)S(1)} %multiply_reduce_fusion.11) | copy-start | bytes 5476
  239.6 129.3 %copy-start.58 = (f32[768]{0:T(1024)S(1)}, f32[768]{0:T(1024)}, u32[]{:S(2)}) copy-start(f32[768]{0:T(1024)} %convert_element_type.363) | copy-start | bytes 9220
  239.6 129.3 %copy-start.66 = (f32[768]{0:T(1024)S(1)}, f32[768]{0:T(1024)}, u32[]{:S(2)}) copy-start(f32[768]{0:T(1024)} %convert_element_type.364) | copy-start | bytes 9220
  239.6 129.3 %copy-start.72 = (f32[768]{0:T(1024)S(1)}, f32[768]{0:T(1024)}, u32[]{:S(2)}) copy-start(f32[768]{0:T(1024)} %convert_element_type.366) | copy-start | bytes 9220
  375.2 217.6 %copy-start.6 = (bf16[456,768]{1,0:T(8,128)(2,1)}, bf16[456,768]{1,0:T(8,128)(2,1)S(1)}, u32[]{:S(2)}) copy-start(bf16[456,768]{1,0:T(8,128)(2,1)S(1)} %add_convert_fusion.4) | copy-start | bytes 2101252
  375.2 105.9 %copy-start.71 = (f32[768]{0:T(1024)S(1)}, f32[768]{0:T(1024)}, u32[]{:S(2)}) copy-start(f32[768]{0:T(1024)} %convert_element_type.370) | copy-start | bytes 9220
  430.8 106.2 %copy-start.70 = (f32[768]{0:T(1024)S(1)}, f32[768]{0:T(1024)}, u32[]{:S(2)}) copy-start(f32[768]{0:T(1024)} %convert_element_type.369) | copy-start | bytes 9220
  557.2 101.7 %copy-start.59 = (f32[768]{0:T(1024)S(1)}, f32[768]{0:T(1024)}, u32[]{:S(2)}) copy-start(f32[768]{0:T(1024)} %convert_element_type.372) | copy-start | bytes 9220
  557.2 101.7 %copy-start.64 = (f32[3072]{0:T(1024)S(1)}, f32[3072]{0:T(1024)}, u32[]{:S(2)}) copy-start(f32[3072]{0:T(1024)} %convert_element_type.374) | copy-start | bytes 36868
  557.2 101.7 %copy-start.67 = (f32[768]{0:T(1024)S(1)}, f32[768]{0:T(1024)}, u32[]{:S(2)}) copy-start(f32[768]{0:T(1024)} %convert_element_type.373) | copy-start | bytes 9220
  596.6 128.1 %copy-start.28 = (f32[456,768]{1,0:T(8,128)S(1)}, f32[456,768]{1,0:T(8,128)}, u32[]{:S(2)}) copy-start(f32[456,768]{1,0:T(8,128)} %copy-done.27) | copy-start | bytes 4202500
  596.6 128.1 %copy-start.68 = (f32[768]{0:T(1024)S(1)}, f32[768]{0:T(1024)}, u32[]{:S(2)}) copy-start(f32[768]{0:T(1024)} %convert_element_type.375) | copy-start | bytes 9220
  (78 other events, 599.4 us)
Sparse Core Ops, SparseCore 0:
  11.5 56.8 all-gather.46
  71.9 52.9 all-gather.44
  128.4 52.9 all-gather.42
  184.1 52.9 all-gather.48
  240.4 62.5 all-gather.50
  306.4 62.4 all-gather.52
  372.3 52.8 all-gather.58
  428.1 52.9 all-gather.56
  484.0 52.9 all-gather.54
  539.8 52.9 all-gather.60
  596.2 62.5 all-gather.62
  662.2 62.4 all-gather.64
  1097.0 807.0 all-reduce.23
where the time goes:
time: 1950 us; the launch traced here: 1930 us
  waiting for transfers between devices  1340 us (69%)
  local copies, waits for them, and re-layouts  329 us (17%)
  matrix products  173 us (9%)
  blocking collectives  43.3 us (2%)
  other arithmetic  34.2 us (2%)
    unnamed x14, waiting for transfers between devices  804 us
    unnamed x267, local copies, waits for them, and re-layouts  178 us
    all_gather x2, waiting for transfers between devices, fetch_forward(): lax.all_gather(shard[9], 'dp', axis=0, tiled=True)  126 us
    all_gather x2, waiting for transfers between devices, fetch_forward(): lax.all_gather(shard[2], 'dp', axis=0, tiled=True)  95.6 us
    all_gather x2, waiting for transfers between devices, fetch_forward(): lax.all_gather(shard[11], 'dp', axis=0, tiled=True)  94.7 us
    all_gather x2, waiting for transfers between devices, fetch_forward(): lax.all_gather(shard[0], 'dp', axis=0, tiled=True)  88.2 us
    all_gather x2, waiting for transfers between devices, fetch_forward(): lax.all_gather(shard[3], 'dp', axis=0, tiled=True)  79.7 us
    dot_general x12, matrix products, dense(): return jnp.dot(left, right, preferred_element_type=jnp.float32)  67.3 us
  transfers between devices with their start and end apart: 13, of which 12 were waited for; matrix products, arithmetic and copies ran while one was open for 7% of the time, Pallas kernels for 0%

commit v1 on v0

v1 whole, which is shorter than its diff:
```python
import functools
import math

import jax
import jax.numpy as jnp
from jax import lax
from jax.experimental import pallas as pl
from jax.experimental.pallas import tpu as pltpu
from jax.sharding import PartitionSpec as P

HEADS = 12
HEAD_DIM = 64
REGIONS = 100

epsilon = 1e-12
F32 = jnp.float32
BF16 = jnp.bfloat16


def rounds_of(owners):
    bits = int(math.log2(owners))
    outer = list(range(3, bits))
    return (outer + [1, 2, 0], outer + [2, 1, 0])


def swaps(owners, step):
    rounds = rounds_of(owners)
    return [(i, i ^ (1 << rounds[i % 2][step])) for i in range(owners)]


def owner_table(owners):
    rounds = rounds_of(owners)
    half = owners // 2
    masks = [
        [sum(((b >> j) & 1) << order[j] for j in range(len(order) - 1)) for b in range(half)]
        for order in rounds
    ]
    me = lax.axis_index("dp")
    core = me % 2
    even, odd = (jnp.array(m, dtype=jnp.int32) for m in masks)
    near = jnp.where(core == 0, even, odd) ^ me
    far = jnp.where(core == 0, odd, even) ^ (me ^ 1)
    return jnp.concatenate([near, far]).astype(jnp.int32)


def tie(value, earlier):
    if earlier is None:
        return value
    return lax.optimization_barrier((value, earlier))[0]


def swap(value, step, owners):
    return lax.ppermute(value, "dp", swaps(owners, step))


class Lane:
    def __init__(self, lag):
        self.lag = lag
        self.ends = []

    def enter(self, value):
        at = len(self.ends) - self.lag
        return tie(value, self.ends[at] if at >= 0 else None)

    def leave(self, value):
        self.ends.append(value)


def gather_piece(shard, owners, lanes):
    steps = int(math.log2(owners)) - 1
    held = shard[None]
    for step in range(steps):
        if step == 0:
            held = lanes[0].enter(held)
        if step == steps - 2:
            held = lanes[1].enter(held)
        came = swap(held, step, owners)
        if step == steps - 3:
            lanes[0].leave(came)
        if step == steps - 1:
            lanes[1].leave(came)
        held = jnp.concatenate([held, came], axis=0)
    return held, swap(held, steps, owners)


def scatter_piece(blocks, owners, lanes):
    steps = int(math.log2(owners))
    held = blocks
    for step in reversed(range(steps)):
        half = held.shape[0] // 2
        if step == steps - 2:
            held = lanes[0].enter(held)
        if step == steps - 4:
            held = lanes[1].enter(held)
        came = swap(held[half:], step, owners)
        if step == steps - 3:
            lanes[0].leave(came)
        if step == 0:
            lanes[1].leave(came)
        held = held[:half].astype(F32) + came.astype(F32)
        if step > 0:
            held = held.astype(BF16)
    return held[0]


def place_kernel(table, *refs, scatter):
    parts, out, sem = refs[:-2], refs[-2], refs[-1]
    copies = []
    b = 0
    for part in parts:
        for j in range(out.shape[0] if scatter else part.shape[0]):
            at = table[b]
            if scatter:
                copies.append(pltpu.make_async_copy(part.at[at], out.at[b], sem.at[b]))
            else:
                copies.append(pltpu.make_async_copy(part.at[j], out.at[at], sem.at[b]))
            copies[-1].start()
            b += 1
    for copy in copies:
        copy.wait()


def place(table, parts, scatter=False):
    owners = table.shape[0]
    shape = (owners,) + parts[0].shape[1:]
    return pl.pallas_call(
        functools.partial(place_kernel, scatter=scatter),
        out_shape=jax.ShapeDtypeStruct(shape, parts[0].dtype),
        in_specs=[pl.BlockSpec(memory_space=pltpu.SMEM)]
        + [pl.BlockSpec(memory_space=pl.ANY)] * len(parts),
        out_specs=pl.BlockSpec(memory_space=pl.ANY),
        scratch_shapes=[pltpu.SemaphoreType.DMA((owners,))],
        cost_estimate=pl.CostEstimate(
            flops=0, bytes_accessed=2 * math.prod(shape) * 2, transcendentals=0
        ),
    )(table, *parts)


def dense(left, right):
    return jnp.dot(left, right, preferred_element_type=F32)


def outer(left, right):
    return lax.dot_general(left, right, (((0,), (0,)), ((), ())), preferred_element_type=F32)


def back_dense(left, right):
    return lax.dot_general(left, right, (((1,), (1,)), ((), ())), preferred_element_type=F32)


def column_sum(values):
    return jnp.sum(values.astype(F32), axis=0)


def slot_valid(region_count, text_mask):
    region_slot = jnp.arange(REGIONS, dtype=jnp.int32)[None, :] < region_count[:, None]
    return jnp.concatenate([text_mask.astype(F32), region_slot.astype(F32)], axis=1)


def norm(values, gain, shift):
    center = values - jnp.mean(values, axis=-1, keepdims=True)
    spread = jnp.mean(center * center, axis=-1, keepdims=True)
    scale = lax.rsqrt(spread + epsilon)
    unit = center * scale
    return unit * gain + shift, (unit, scale)


def norm_back(saved, gain, grad):
    unit, scale = saved
    inner = grad * gain
    into = scale * (
        inner
        - jnp.mean(inner, axis=-1, keepdims=True)
        - unit * jnp.mean(inner * unit, axis=-1, keepdims=True)
    )
    return into, column_sum(grad * unit), column_sum(grad)


def forward_layer(inputs, weights, vectors, valid_keys):
    q_weight, k_weight, v_weight, o_weight, up_weight, down_weight = weights
    q_bias, v_bias, o_bias, gain_one, shift_one, up_bias, down_bias, gain_two, shift_two = vectors
    item_count = valid_keys.shape[0]
    row_count, width = inputs.shape

    def heads_of(values):
        return values.reshape(item_count, row_count // item_count, HEADS, HEAD_DIM)

    queries = heads_of((dense(inputs, q_weight) + q_bias).astype(BF16))
    key_rows = heads_of(dense(inputs, k_weight).astype(BF16))
    value_rows = heads_of((dense(inputs, v_weight) + v_bias).astype(BF16))
    scores = (
        jnp.einsum("bqhd,bkhd->bhqk", queries, key_rows, preferred_element_type=F32) * 0.125
    )
    scores = scores + (valid_keys[:, None, None, :] - 1.0) * 10000.0
    attention = jax.nn.softmax(scores, axis=-1)
    attention_low = attention.astype(BF16)
    context = jnp.einsum("bhqk,bkhd->bqhd", attention_low, value_rows, preferred_element_type=F32)
    context = context.astype(BF16).reshape(row_count, width)
    first_sum = inputs.astype(F32) + dense(context, o_weight) + o_bias
    middle, norm_one = norm(first_sum, gain_one, shift_one)
    middle = middle.astype(BF16)
    lifted = dense(middle, up_weight) + up_bias
    half = 0.5 * lax.erf(lifted * math.sqrt(0.5)) + 0.5
    activated = (lifted * half).astype(BF16)
    slope = half + lifted * jnp.exp(-0.5 * lifted * lifted) * (1.0 / math.sqrt(2.0 * math.pi))
    slope = slope.astype(BF16)
    second_sum = middle.astype(F32) + dense(activated, down_weight) + down_bias
    output, norm_two = norm(second_sum, gain_two, shift_two)
    saved = (queries, key_rows, value_rows, attention, attention_low, context, norm_one, middle, slope, activated, norm_two)
    return output.astype(BF16), saved


def backward_layer(inputs, weights, vectors, saved, out_grad, send):
    q_weight, k_weight, v_weight, o_weight, up_weight, down_weight = weights
    q_bias, v_bias, o_bias, gain_one, shift_one, up_bias, down_bias, gain_two, shift_two = vectors
    queries, key_rows, value_rows, attention, attention_low, context, norm_one, middle, slope, activated, norm_two = saved
    row_count, width = inputs.shape
    sum_grad, gain_two_grad, shift_two_grad = norm_back(norm_two, gain_two, out_grad)
    lowered_grad = sum_grad.astype(BF16)
    send("down", [outer(activated, lowered_grad)])
    lifted_grad = (back_dense(lowered_grad, down_weight) * slope).astype(BF16)
    send("up", [outer(middle, lifted_grad)])
    middle_grad = sum_grad + back_dense(lifted_grad, up_weight)
    first_grad, gain_one_grad, shift_one_grad = norm_back(norm_one, gain_one, middle_grad)
    attended_grad = first_grad.astype(BF16)
    o_grad = outer(context, attended_grad)
    context_grad = back_dense(attended_grad, o_weight).astype(BF16).reshape(queries.shape)
    attention_grad = jnp.einsum(
        "bqhd,bkhd->bhqk", context_grad, value_rows, preferred_element_type=F32
    )
    value_grad = jnp.einsum(
        "bhqk,bqhd->bkhd", attention_low, context_grad, preferred_element_type=F32
    )
    value_grad = value_grad.astype(BF16).reshape(row_count, width)
    weighed = attention * attention_grad
    score_grad = (weighed - attention * jnp.sum(weighed, axis=-1, keepdims=True)).astype(BF16)
    query_grad = (
        jnp.einsum("bhqk,bkhd->bqhd", score_grad, key_rows, preferred_element_type=F32) * 0.125
    )
    query_grad = query_grad.astype(BF16).reshape(row_count, width)
    key_grad = (
        jnp.einsum("bhqk,bqhd->bkhd", score_grad, queries, preferred_element_type=F32) * 0.125
    )
    key_grad = key_grad.astype(BF16).reshape(row_count, width)
    send("four", [outer(inputs, query_grad), outer(inputs, key_grad), outer(inputs, value_grad), o_grad])
    input_grad = (
        first_grad
        + back_dense(query_grad, q_weight)
        + back_dense(key_grad, k_weight)
        + back_dense(value_grad, v_weight)
    )
    small = (column_sum(query_grad), column_sum(value_grad), column_sum(attended_grad), gain_one_grad, shift_one_grad, column_sum(lifted_grad), column_sum(lowered_grad), gain_two_grad, shift_two_grad)
    return input_grad, small


def shards(
    hidden, region_count, text_mask,
    q_weight, k_weight, v_weight, o_weight, q_bias, v_bias, o_bias, gain_one, shift_one,
    up_weight, up_bias, down_weight, down_bias, gain_two, shift_two, cotangent,
):
    owners = lax.axis_size("dp")
    layers = q_weight.shape[0]
    valid_keys = slot_valid(region_count, text_mask)
    doubling = owners >= 16 and owners & (owners - 1) == 0 and q_weight.shape[1] % 8 == 0
    table = owner_table(owners) if doubling else None

    small = (q_bias, v_bias, o_bias, gain_one, shift_one, up_bias, down_bias, gain_two, shift_two)
    packed = jnp.concatenate([v.reshape(1, -1) for v in small], axis=1)
    packed = lax.all_gather(packed, "dp", axis=0, tiled=True).astype(F32)
    vectors = []
    offset = 0
    for v in small:
        size = v.shape[0] * v.shape[1]
        part = packed[:, offset : offset + size].reshape((owners,) + v.shape)
        vectors.append(jnp.swapaxes(part, 0, 1).reshape(layers, -1))
        offset += size
    vectors = [tuple(v[layer] for v in vectors) for layer in range(layers)]

    def whole(blocks):
        return blocks.reshape((-1, blocks.shape[-1]))

    lanes = (Lane(3), Lane(3))
    gathered = []
    for layer in range(layers):
        four = [w[layer] for w in (q_weight, k_weight, v_weight, o_weight)]
        if not doubling:
            gathered.append(
                tuple(
                    lax.all_gather(w, "dp", axis=0, tiled=True)
                    for w in four + [up_weight[layer], down_weight[layer]]
                )
            )
            continue
        rows = four[0].shape[0]
        near, far = gather_piece(jnp.stack(four), owners, lanes)
        fours = [place(table, [near[:, i], far[:, i]]) for i in range(4)]
        up = place(table, list(gather_piece(up_weight[layer], owners, lanes)))
        down = place(table, list(gather_piece(down_weight[layer], owners, lanes)))
        gathered.append(tuple(whole(w) for w in fours + [up, down]))

    current = hidden
    inputs, saved = [], []
    for layer in range(layers):
        inputs.append(current)
        current, kept = forward_layer(current, gathered[layer], vectors[layer], valid_keys)
        saved.append(kept)
    flowing = cotangent.astype(F32)
    lanes = (Lane(2), Lane(2))
    big = [{} for _ in range(layers)]
    tiny = [None] * layers
    for layer in reversed(range(layers)):

        def send(name, grads, layer=layer):
            lows = [g.astype(BF16).reshape(owners, -1, g.shape[-1]) for g in grads]
            if not doubling:
                big[layer][name] = [
                    lax.psum_scatter(g, "dp", scatter_dimension=0, tiled=True)[0].astype(F32)
                    for g in lows
                ]
                return
            lows = [place(table, [g], scatter=True) for g in lows]
            rows = lows[0].shape[1]
            mine = scatter_piece(jnp.concatenate(lows, axis=1) if len(lows) > 1 else lows[0], owners, lanes)
            big[layer][name] = [mine[i * rows : (i + 1) * rows] for i in range(len(lows))]

        flowing, tiny[layer] = backward_layer(
            inputs[layer], gathered[layer], vectors[layer], saved[layer], flowing, send
        )
    sizes = [v.shape[1] for v in small]
    flat = jnp.concatenate(
        [g.reshape(owners, -1) for layer in range(layers) for g in tiny[layer]], axis=1
    )
    flat = lax.psum_scatter(flat, "dp", scatter_dimension=0, tiled=True).reshape(layers, -1)
    summed = []
    offset = 0
    for size in sizes:
        summed.append(flat[:, offset : offset + size])
        offset += size
    q_b, v_b, o_b, g_one, s_one, u_b, d_b, g_two, s_two = summed
    fours = [jnp.stack([big[layer]["four"][i] for layer in range(layers)]) for i in range(4)]
    up = jnp.stack([big[layer]["up"][0] for layer in range(layers)])
    down = jnp.stack([big[layer]["down"][0] for layer in range(layers)])
    return (
        current, flowing, fours[0], fours[1], fours[2], fours[3],
        q_b, v_b, o_b, g_one, s_one, up, u_b, down, d_b, g_two, s_two,
    )


def solution(mesh):
    rows = P("dp", None)
    matrix = P(None, "dp", None)
    vector = P(None, "dp")
    four = (matrix,) * 4
    return jax.shard_map(
        shards,
        mesh=mesh,
        in_specs=(rows, P("dp"), rows) + four + (vector,) * 5
        + (matrix, vector, matrix, vector, vector, vector, rows),
        out_specs=(rows, rows) + four + (vector,) * 5
        + (matrix, vector, matrix, vector, vector, vector),
        check_vma=False,
    )
```

time: 1950 us -> 2470 us (1.27)
  Pallas kernels: 0 us -> 1770 us
  waiting for transfers between devices: 1340 us -> 267 us
  local copies, waits for them, and re-layouts: 329 us -> 137 us
  starting transfers between devices: 0.52 us -> 38.7 us
  matrix products: 173 us -> 145 us
    pallas_call x0 -> x24, Pallas kernels: none -> 1770 us  [place(): pl.pallas_call(functools.partial(place_kernel, scatter=scatter), out_shap...]
    unnamed x14 -> x2, waiting for transfers between devices: 804 us -> 0.04 us
    all_gather x12 -> x0, waiting for transfers between devices: 534 us -> none  [the longest x2 126 us: fetch_forward(): lax.all_gather(shard[9], 'dp', axis=0, tiled=True)]
    ppermute x0 -> x60, waiting for transfers between devices: none -> 267 us  [swap(): return lax.ppermute(value, 'dp', swaps(owners, step))]
    unnamed x267 -> x264, local copies, waits for them, and re-layouts: 178 us -> 17.3 us
    reshape x46 -> x45, local copies, waits for them, and re-layouts: 91.8 us -> 27.5 us  [the longest x2 6.82 us: backward_layer(): query_grad = query_grad.astype(BF16).reshape(row_count, width)]
    unnamed x1 -> x0, blocking collectives: 43.3 us -> none
    all_gather x0 -> x1, blocking collectives: none -> 43.2 us  [shards(): packed = lax.all_gather(packed, 'dp', axis=0, tiled=True).astype(F32)]
  transfers between devices with their start and end apart: 13 -> 61, of which waited for: 12 -> 29; matrix products, arithmetic and copies ran while one was open for 7% -> 8% of each run, Pallas kernels for 0% -> 60%
where the time goes in v1:
time: 2470 us; the launch traced here: 2460 us
  Pallas kernels  1770 us (72%)
  waiting for transfers between devices  267 us (11%)
  matrix products  145 us (6%)
  local copies, waits for them, and re-layouts  137 us (6%)
  other arithmetic  44.3 us (2%)
  blocking collectives  43.2 us (2%)
  starting transfers between devices  38.7 us (2%)
    pallas_call x24, Pallas kernels, place(): pl.pallas_call(functools.partial(place_kernel, scatter=scatter), out_shap...  1770 us
    ppermute x60, waiting for transfers between devices, swap(): return lax.ppermute(value, 'dp', swaps(owners, step))  267 us
  transfers between devices with their start and end apart: 61, of which 29 were waited for; matrix products, arithmetic and copies ran while one was open for 8% of the time, Pallas kernels for 60%

profile of v1, /device:TPU:0, one launch (start us, length us, event | category | flops | bytes accessed | tf_op | source)
XLA Modules:
  0.0 2458.6 jit_solution(15124307870276135321)
XLA Ops:
  23.2 43.2 %all-gather = bf16[32,1,576]{2,1,0:T(2,128)(2,1)} all-gather(bf16[1,1,576]{2,1,0:T(2,128)(2,1)S(1)} %bitcast.282), channel_id=1, replica_groups=mesh['dp'=32] {'dp'}, dimensions={0}, use_global_device_ids=true | all-gather | bytes 38016 | tf_op jit(solution)/shard_map/all_gather | solution.py:269
  112.2 19.3 collective-permute-done.11
  158.1 32.7 %collective-permute-done.21 = bf16[2,24,3072]{2,1,0:T(8,128)(2,1)S(1)} collective-permute-done((bf16[2,24,3072]{2,1,0:T(8,128)(2,1)S(1)}, bf16[2,24,3072]{2,1,0:T(8,128)(2,1)S(1)}, u32[]{:S(2)}, u32[]{:S(2)}) %collective-permute-start.21) | collective-permute-done | bytes 294944 | tf_op jit(solution)/shard_map/ppermute | solution.py:53
  195.3 18.2 collective-permute-done.8
  214.4 18.1 collective-permute-done.3
  287.1 37.9 %shard_map.333 = bf16[32,24,768]{2,1,0:T(8,128)(2,1)} custom-call(s32[32]{0:T(128)} %pad_add_fusion.table, bf16[16,24,768]{2,1,0:T(8,128)(2,1)} %get-tuple-element.83.refs_0_, bf16[16,24,768]{2,1,0:T(8,128)(2,1)} %get-tuple-element.79.refs_1_), custom_call_target="tpu_custom_call" | custom-call | bytes 2359296 | tf_op jit(solution)/shard_map/pallas_call | solution.py:126
  327.8 37.8 %shard_map.334 = bf16[32,24,768]{2,1,0:T(8,128)(2,1)} custom-call(s32[32]{0:T(128)} %pad_add_fusion.table, bf16[16,24,768]{2,1,0:T(8,128)(2,1)} %get-tuple-element.82.refs_0_, bf16[16,24,768]{2,1,0:T(8,128)(2,1)} %get-tuple-element.78.refs_1_), custom_call_target="tpu_custom_call" | custom-call | bytes 2359296 | tf_op jit(solution)/shard_map/pallas_call | solution.py:126
  368.3 37.9 %shard_map.332 = bf16[32,24,768]{2,1,0:T(8,128)(2,1)} custom-call(s32[32]{0:T(128)} %pad_add_fusion.table, bf16[16,24,768]{2,1,0:T(8,128)(2,1)} %get-tuple-element.84.refs_0_, bf16[16,24,768]{2,1,0:T(8,128)(2,1)} %get-tuple-element.80.refs_1_), custom_call_target="tpu_custom_call" | custom-call | bytes 2359296 | tf_op jit(solution)/shard_map/pallas_call | solution.py:126
  419.4 37.8 %shard_map.335 = bf16[32,24,768]{2,1,0:T(8,128)(2,1)} custom-call(s32[32]{0:T(128)} %pad_add_fusion.table, bf16[16,24,768]{2,1,0:T(8,128)(2,1)} %get-tuple-element.81.refs_0_, bf16[16,24,768]{2,1,0:T(8,128)(2,1)} %get-tuple-element.77.refs_1_), custom_call_target="tpu_custom_call" | custom-call | bytes 2359296 | tf_op jit(solution)/shard_map/pallas_call | solution.py:126
  457.2 145.1 %shard_map.336 = bf16[32,24,3072]{2,1,0:T(8,128)(2,1)} custom-call(s32[32]{0:T(128)} %pad_add_fusion.table, bf16[16,24,3072]{2,1,0:T(8,128)(2,1)} %constant_dynamic-update-slice_fusion.5.refs_0_, bf16[16,24,3072]{2,1,0:T(8,128)(2,1)} %collective-permute-done.9.refs_1_), custom_call_target="tpu_custom_call" | custom-call | bytes 9437184 | tf_op jit(solution)/shard_map/pallas_call | solution.py:126
  605.1 145.1 %shard_map.337 = bf16[32,96,768]{2,1,0:T(8,128)(2,1)} custom-call(s32[32]{0:T(128)} %pad_add_fusion.table, bf16[16,96,768]{2,1,0:T(8,128)(2,1)} %constant_dynamic-update-slice_fusion.10.refs_0_, bf16[16,96,768]{2,1,0:T(8,128)(2,1)} %collective-permute-done.14.refs_1_), custom_call_target="tpu_custom_call" | custom-call | bytes 9437184 | tf_op jit(solution)/shard_map/pallas_call | solution.py:126
  763.5 37.9 %shard_map.339 = bf16[32,24,768]{2,1,0:T(8,128)(2,1)} custom-call(s32[32]{0:T(128)} %pad_add_fusion.table, bf16[16,24,768]{2,1,0:T(8,128)(2,1)} %get-tuple-element.75.refs_0_, bf16[16,24,768]{2,1,0:T(8,128)(2,1)} %get-tuple-element.71.refs_1_), custom_call_target="tpu_custom_call" | custom-call | bytes 2359296 | tf_op jit(solution)/shard_map/pallas_call | solution.py:126
  804.2 37.9 %shard_map.340 = bf16[32,24,768]{2,1,0:T(8,128)(2,1)} custom-call(s32[32]{0:T(128)} %pad_add_fusion.table, bf16[16,24,768]{2,1,0:T(8,128)(2,1)} %get-tuple-element.74.refs_0_, bf16[16,24,768]{2,1,0:T(8,128)(2,1)} %get-tuple-element.70.refs_1_), custom_call_target="tpu_custom_call" | custom-call | bytes 2359296 | tf_op jit(solution)/shard_map/pallas_call | solution.py:126
  847.7 37.9 %shard_map.338 = bf16[32,24,768]{2,1,0:T(8,128)(2,1)} custom-call(s32[32]{0:T(128)} %pad_add_fusion.table, bf16[16,24,768]{2,1,0:T(8,128)(2,1)} %get-tuple-element.76.refs_0_, bf16[16,24,768]{2,1,0:T(8,128)(2,1)} %get-tuple-element.72.refs_1_), custom_call_target="tpu_custom_call" | custom-call | bytes 2359296 | tf_op jit(solution)/shard_map/pallas_call | solution.py:126
  902.7 37.8 %shard_map.341 = bf16[32,24,768]{2,1,0:T(8,128)(2,1)} custom-call(s32[32]{0:T(128)} %pad_add_fusion.table, bf16[16,24,768]{2,1,0:T(8,128)(2,1)} %get-tuple-element.73.refs_0_, bf16[16,24,768]{2,1,0:T(8,128)(2,1)} %get-tuple-element.69.refs_1_), custom_call_target="tpu_custom_call" | custom-call | bytes 2359296 | tf_op jit(solution)/shard_map/pallas_call | solution.py:126
  940.5 145.1 %shard_map.342 = bf16[32,24,3072]{2,1,0:T(8,128)(2,1)} custom-call(s32[32]{0:T(128)} %pad_add_fusion.table, bf16[16,24,3072]{2,1,0:T(8,128)(2,1)} %constant_dynamic-update-slice_fusion.18.refs_0_, bf16[16,24,3072]{2,1,0:T(8,128)(2,1)} %collective-permute-done.24.refs_1_), custom_call_target="tpu_custom_call" | custom-call | bytes 9437184 | tf_op jit(solution)/shard_map/pallas_call | solution.py:126
  1094.5 145.0 %shard_map.343 = bf16[32,96,768]{2,1,0:T(8,128)(2,1)} custom-call(s32[32]{0:T(128)} %pad_add_fusion.table, bf16[16,96,768]{2,1,0:T(8,128)(2,1)} %constant_dynamic-update-slice_fusion.21.refs_0_, bf16[16,96,768]{2,1,0:T(8,128)(2,1)} %collective-permute-done.29.refs_1_), custom_call_target="tpu_custom_call" | custom-call | bytes 9437184 | tf_op jit(solution)/shard_map/pallas_call | solution.py:126
  1352.1 145.0 %shard_map.349 = bf16[32,24,3072]{2,1,0:T(8,128)(2,1)} custom-call(s32[32]{0:T(128)} %pad_add_fusion.table, bf16[32,24,3072]{2,1,0:T(8,128)(2,1)} %bitcast.240), custom_call_target="tpu_custom_call" | custom-call | bytes 9437184 | tf_op jit(solution)/shard_map/pallas_call | solution.py:126
  1500.4 145.0 %shard_map.348 = bf16[32,96,768]{2,1,0:T(8,128)(2,1)} custom-call(s32[32]{0:T(128)} %pad_add_fusion.table, bf16[32,96,768]{2,1,0:T(8,128)(2,1)} %bitcast.243), custom_call_target="tpu_custom_call" | custom-call | bytes 9437184 | tf_op jit(solution)/shard_map/pallas_call | solution.py:126
  1649.1 145.0 %shard_map.354 = bf16[32,96,768]{2,1,0:T(8,128)(2,1)} custom-call(s32[32]{0:T(128)} %pad_add_fusion.table, bf16[32,96,768]{2,1,0:T(8,128)(2,1)} %bitcast.241), custom_call_target="tpu_custom_call" | custom-call | bytes 9437184 | tf_op jit(solution)/shard_map/pallas_call | solution.py:126
  1797.4 145.0 %shard_map.355 = bf16[32,24,3072]{2,1,0:T(8,128)(2,1)} custom-call(s32[32]{0:T(128)} %pad_add_fusion.table, bf16[32,24,3072]{2,1,0:T(8,128)(2,1)} %bitcast.242), custom_call_target="tpu_custom_call" | custom-call | bytes 9437184 | tf_op jit(solution)/shard_map/pallas_call | solution.py:126
  1946.1 37.8 %shard_map.350 = bf16[32,24,768]{2,1,0:T(8,128)(2,1)} custom-call(s32[32]{0:T(128)} %pad_add_fusion.table, bf16[32,24,768]{2,1,0:T(8,128)(2,1)} %bitcast.264), custom_call_target="tpu_custom_call" | custom-call | bytes 2359296 | tf_op jit(solution)/shard_map/pallas_call | solution.py:126
  1983.9 37.8 %shard_map.351 = bf16[32,24,768]{2,1,0:T(8,128)(2,1)} custom-call(s32[32]{0:T(128)} %pad_add_fusion.table, bf16[32,24,768]{2,1,0:T(8,128)(2,1)} %bitcast.265), custom_call_target="tpu_custom_call" | custom-call | bytes 2359296 | tf_op jit(solution)/shard_map/pallas_call | solution.py:126
  2021.7 37.8 %shard_map.352 = bf16[32,24,768]{2,1,0:T(8,128)(2,1)} custom-call(s32[32]{0:T(128)} %pad_add_fusion.table, bf16[32,24,768]{2,1,0:T(8,128)(2,1)} %bitcast.266), custom_call_target="tpu_custom_call" | custom-call | bytes 2359296 | tf_op jit(solution)/shard_map/pallas_call | solution.py:126
  2059.5 37.9 %shard_map.353 = bf16[32,24,768]{2,1,0:T(8,128)(2,1)} custom-call(s32[32]{0:T(128)} %pad_add_fusion.table, bf16[32,24,768]{2,1,0:T(8,128)(2,1)} %bitcast.231), custom_call_target="tpu_custom_call" | custom-call | bytes 2359296 | tf_op jit(solution)/shard_map/pallas_call | solution.py:126
  2125.0 37.8 %shard_map.347 = bf16[32,24,768]{2,1,0:T(8,128)(2,1)} custom-call(s32[32]{0:T(128)} %pad_add_fusion.table, bf16[32,24,768]{2,1,0:T(8,128)(2,1)} %bitcast.230), custom_call_target="tpu_custom_call" | custom-call | bytes 2359296 | tf_op jit(solution)/shard_map/pallas_call | solution.py:126
  2162.8 37.8 %shard_map.346 = bf16[32,24,768]{2,1,0:T(8,128)(2,1)} custom-call(s32[32]{0:T(128)} %pad_add_fusion.table, bf16[32,24,768]{2,1,0:T(8,128)(2,1)} %bitcast.271), custom_call_target="tpu_custom_call" | custom-call | bytes 2359296 | tf_op jit(solution)/shard_map/pallas_call | solution.py:126
  2200.6 37.8 %shard_map.345 = bf16[32,24,768]{2,1,0:T(8,128)(2,1)} custom-call(s32[32]{0:T(128)} %pad_add_fusion.table, bf16[32,24,768]{2,1,0:T(8,128)(2,1)} %bitcast.269), custom_call_target="tpu_custom_call" | custom-call | bytes 2359296 | tf_op jit(solution)/shard_map/pallas_call | solution.py:126
  2238.4 37.9 %shard_map.344 = bf16[32,24,768]{2,1,0:T(8,128)(2,1)} custom-call(s32[32]{0:T(128)} %pad_add_fusion.table, bf16[32,24,768]{2,1,0:T(8,128)(2,1)} %bitcast.270), custom_call_target="tpu_custom_call" | custom-call | bytes 2359296 | tf_op jit(solution)/shard_map/pallas_call | solution.py:126
  2308.3 15.8 collective-permute-done.47
  2378.1 16.3 collective-permute-done.53
  2421.7 13.6 collective-permute-done.43
  (689 shorter events, 498.1 us)
Async XLA Ops:
  7.2 2275.3 %all-reduce.3.cloned.1.call-start = ((), (), s32[]{:S(2)}) async-start(), calls=%async_computation | async-start | bytes 163840
  9.0 98.6 %collective-permute-start.10 = (bf16[1,96,768]{2,1,0:T(8,128)(2,1)S(1)}, bf16[1,96,768]{2,1,0:T(8,128)(2,1)S(1)}, u32[]{:S(2)}, u32[]{:S(2)}) collective-permute-start(bf16[1,96,768]{2,1,0:T(8,128)(2,1)S(1)} %get-tuple-element.96), channel_id=1, source_target_pairs={{0,8},{1,9},{2,10},{3,11},{4,12},{5,13},{6,14},{7,15},{8,0},{9,1},... | collective-permute-start | bytes 442376 | tf_op jit(solution)/shard_map/ppermute | solution.py:53
  15.0 92.8 %collective-permute-start = (bf16[1,4,24,768]{3,2,0,1:T(8,128)(2,1)S(1)}, bf16[1,4,24,768]{3,2,0,1:T(8,128)(2,1)S(1)}, u32[]{:S(2)}, u32[]{:S(2)}) collective-permute-start(bf16[1,4,24,768]{3,2,0,1:T(8,128)(2,1)S(1)} %maximum_bitcast_fusion), channel_id=1, source_target_pairs={{0,8},{1,9},{2,10},{3,11},{4,12},{5,13},{6,14},{7,15},{8,0},{9,1},... | collective-permute-start | bytes 442376 | tf_op jit(solution)/shard_map/ppermute | solution.py:53
  15.8 94.9 %collective-permute-start.5 = (bf16[1,24,3072]{2,1,0:T(8,128)(2,1)S(1)}, bf16[1,24,3072]{2,1,0:T(8,128)(2,1)S(1)}, u32[]{:S(2)}, u32[]{:S(2)}) collective-permute-start(bf16[1,24,3072]{2,1,0:T(8,128)(2,1)S(1)} %get-tuple-element.99), channel_id=1, source_target_pairs={{0,8},{1,9},{2,10},{3,11},{4,12},{5,13},{6,14},{7,15},{8,0},{9,1},... | collective-permute-start | bytes 442376 | tf_op jit(solution)/shard_map/ppermute | solution.py:53
  107.8 30.1 %collective-permute-start.1 = (bf16[2,4,24,768]{3,2,0,1:T(8,128)(2,1)S(1)}, bf16[2,4,24,768]{3,2,0,1:T(8,128)(2,1)S(1)}, u32[]{:S(2)}, u32[]{:S(2)}) collective-permute-start(bf16[2,4,24,768]{3,2,0,1:T(8,128)(2,1)S(1)} %pad_maximum_fusion.16), channel_id=1, source_target_pairs={{0,16},{1,17},{2,18},{3,19},{4,20},{5,21},{6,22},{7,23},{8,24},{9,... | collective-permute-start | bytes 884744 | tf_op jit(solution)/shard_map/ppermute | solution.py:53
  110.8 33.4 %collective-permute-start.6 = (bf16[2,24,3072]{2,1,0:T(8,128)(2,1)S(1)}, bf16[2,24,3072]{2,1,0:T(8,128)(2,1)S(1)}, u32[]{:S(2)}, u32[]{:S(2)}) collective-permute-start(bf16[2,24,3072]{2,1,0:T(8,128)(2,1)S(1)} %pad_maximum_fusion.17), channel_id=1, source_target_pairs={{0,16},{1,17},{2,18},{3,19},{4,20},{5,21},{6,22},{7,23},{8,24},{9,... | collective-permute-start | bytes 884744 | tf_op jit(solution)/shard_map/ppermute | solution.py:53
  138.0 55.1 %collective-permute-start.2 = (bf16[4,4,24,768]{3,2,0,1:T(8,128)(2,1)S(1)}, bf16[4,4,24,768]{3,2,0,1:T(8,128)(2,1)S(1)}, u32[]{:S(2)}, u32[]{:S(2)}) collective-permute-start(bf16[4,4,24,768]{3,2,0,1:T(8,128)(2,1)S(1)} %pad_maximum_fusion.8), channel_id=1, source_target_pairs={{0,2},{1,5},{2,0},{3,7},{4,6},{5,1},{6,4},{7,3},{8,10},{9,13},{10,... | collective-permute-start | bytes 1769480 | tf_op jit(solution)/shard_map/ppermute | solution.py:53
  150.5 42.8 %collective-permute-start.26 = (bf16[2,96,768]{2,1,0:T(8,128)(2,1)S(1)}, bf16[2,96,768]{2,1,0:T(8,128)(2,1)S(1)}, u32[]{:S(2)}, u32[]{:S(2)}) collective-permute-start(bf16[2,96,768]{2,1,0:T(8,128)(2,1)S(1)} %pad_maximum_fusion.21), channel_id=1, source_target_pairs={{0,16},{1,17},{2,18},{3,19},{4,20},{5,21},{6,22},{7,23},{8,24},{9,... | collective-permute-start | bytes 884744 | tf_op jit(solution)/shard_map/ppermute | solution.py:53
  153.5 39.8 %collective-permute-start.16 = (bf16[2,4,24,768]{3,2,0,1:T(8,128)(2,1)S(1)}, bf16[2,4,24,768]{3,2,0,1:T(8,128)(2,1)S(1)}, u32[]{:S(2)}, u32[]{:S(2)}) collective-permute-start(bf16[2,4,24,768]{3,2,0,1:T(8,128)(2,1)S(1)} %pad_maximum_fusion.19), channel_id=1, source_target_pairs={{0,16},{1,17},{2,18},{3,19},{4,20},{5,21},{6,22},{7,23},{8,24},{9,... | collective-permute-start | bytes 884744 | tf_op jit(solution)/shard_map/ppermute | solution.py:53
  153.6 37.2 %collective-permute-start.21 = (bf16[2,24,3072]{2,1,0:T(8,128)(2,1)S(1)}, bf16[2,24,3072]{2,1,0:T(8,128)(2,1)S(1)}, u32[]{:S(2)}, u32[]{:S(2)}) collective-permute-start(bf16[2,24,3072]{2,1,0:T(8,128)(2,1)S(1)} %pad_maximum_fusion.20), channel_id=1, source_target_pairs={{0,16},{1,17},{2,18},{3,19},{4,20},{5,21},{6,22},{7,23},{8,24},{9,... | collective-permute-start | bytes 884744 | tf_op jit(solution)/shard_map/ppermute | solution.py:53
  156.7 38.6 %collective-permute-start.13 = (bf16[8,96,768]{2,1,0:T(8,128)(2,1)S(1)}, bf16[8,96,768]{2,1,0:T(8,128)(2,1)S(1)}, u32[]{:S(2)}, u32[]{:S(2)}) collective-permute-start(bf16[8,96,768]{2,1,0:T(8,128)(2,1)S(1)} %pad_maximum_fusion.4), channel_id=1, source_target_pairs={{0,4},{1,3},{2,6},{3,1},{4,0},{5,7},{6,2},{7,5},{8,12},{9,11},{10,... | collective-permute-start | bytes 3538952 | tf_op jit(solution)/shard_map/ppermute | solution.py:53
  193.2 39.3 %collective-permute-start.3 = (bf16[8,4,24,768]{3,2,0,1:T(8,128)(2,1)S(1)}, bf16[8,4,24,768]{3,2,0,1:T(8,128)(2,1)S(1)}, u32[]{:S(2)}, u32[]{:S(2)}) collective-permute-start(bf16[8,4,24,768]{3,2,0,1:T(8,128)(2,1)S(1)} %pad_maximum_fusion.2), channel_id=1, source_target_pairs={{0,4},{1,3},{2,6},{3,1},{4,0},{5,7},{6,2},{7,5},{8,12},{9,11},{10,... | collective-permute-start | bytes 3538952 | tf_op jit(solution)/shard_map/ppermute | solution.py:53
  195.3 49.3 %collective-permute-start.27 = (bf16[4,96,768]{2,1,0:T(8,128)(2,1)S(1)}, bf16[4,96,768]{2,1,0:T(8,128)(2,1)S(1)}, u32[]{:S(2)}, u32[]{:S(2)}) collective-permute-start(bf16[4,96,768]{2,1,0:T(8,128)(2,1)S(1)} %pad_maximum_fusion.13), channel_id=1, source_target_pairs={{0,2},{1,5},{2,0},{3,7},{4,6},{5,1},{6,4},{7,3},{8,10},{9,13},{10,... | collective-permute-start | bytes 1769480 | tf_op jit(solution)/shard_map/ppermute | solution.py:53
  213.5 32.1 %collective-permute-start.22 = (bf16[4,24,3072]{2,1,0:T(8,128)(2,1)S(1)}, bf16[4,24,3072]{2,1,0:T(8,128)(2,1)S(1)}, u32[]{:S(2)}, u32[]{:S(2)}) collective-permute-start(bf16[4,24,3072]{2,1,0:T(8,128)(2,1)S(1)} %pad_maximum_fusion.12), channel_id=1, source_target_pairs={{0,2},{1,5},{2,0},{3,7},{4,6},{5,1},{6,4},{7,3},{8,10},{9,13},{10,... | collective-permute-start | bytes 1769480 | tf_op jit(solution)/shard_map/ppermute | solution.py:53
  232.6 52.6 %collective-permute-start.4 = (bf16[16,4,24,768]{3,2,0,1:T(8,128)(2,1)S(1)}, bf16[16,4,24,768]{3,2,0,1:T(8,128)(2,1)S(1)}, u32[]{:S(2)}, u32[]{:S(2)}) collective-permute-start(bf16[16,4,24,768]{3,2,0,1:T(8,128)(2,1)S(1)} %constant_dynamic-update-slice_fusion), channel_id=1, source_target_pairs={{0,1},{1,0},{2,3},{3,2},{4,5},{5,4},{6,7},{7,6},{8,9},{9,8},{10,11... | collective-permute-start | bytes 7077896 | tf_op jit(solution)/shard_map/ppermute | solution.py:53
  236.9 220.3 %collective-permute-start.9 = (bf16[16,24,3072]{2,1,0:T(8,128)(2,1)}, bf16[16,24,3072]{2,1,0:T(8,128)(2,1)}, u32[]{:S(2)}, u32[]{:S(2)}) collective-permute-start(bf16[16,24,3072]{2,1,0:T(8,128)(2,1)} %constant_dynamic-update-slice_fusion.5.refs_0_), channel_id=1, source_target_pairs={{0,1},{1,0},{2,3},{3,2},{4,5},{5,4},{6,7},{7,6},{8,9},{9,8},{10,11... | collective-permute-start | bytes 7077896 | tf_op jit(solution)/shard_map/ppermute | solution.py:53
  244.7 26.7 %collective-permute-start.28 = (bf16[8,96,768]{2,1,0:T(8,128)(2,1)S(1)}, bf16[8,96,768]{2,1,0:T(8,128)(2,1)S(1)}, u32[]{:S(2)}, u32[]{:S(2)}) collective-permute-start(bf16[8,96,768]{2,1,0:T(8,128)(2,1)S(1)} %pad_maximum_fusion.7), channel_id=1, source_target_pairs={{0,4},{1,3},{2,6},{3,1},{4,0},{5,7},{6,2},{7,5},{8,12},{9,11},{10,... | collective-permute-start | bytes 3538952 | tf_op jit(solution)/shard_map/ppermute | solution.py:53
  245.8 38.3 %collective-permute-start.23 = (bf16[8,24,3072]{2,1,0:T(8,128)(2,1)S(1)}, bf16[8,24,3072]{2,1,0:T(8,128)(2,1)S(1)}, u32[]{:S(2)}, u32[]{:S(2)}) collective-permute-start(bf16[8,24,3072]{2,1,0:T(8,128)(2,1)S(1)} %pad_maximum_fusion.6), channel_id=1, source_target_pairs={{0,4},{1,3},{2,6},{3,1},{4,0},{5,7},{6,2},{7,5},{8,12},{9,11},{10,... | collective-permute-start | bytes 3538952 | tf_op jit(solution)/shard_map/ppermute | solution.py:53
  258.7 346.3 %collective-permute-start.14 = (bf16[16,96,768]{2,1,0:T(8,128)(2,1)}, bf16[16,96,768]{2,1,0:T(8,128)(2,1)}, u32[]{:S(2)}, u32[]{:S(2)}) collective-permute-start(bf16[16,96,768]{2,1,0:T(8,128)(2,1)} %constant_dynamic-update-slice_fusion.10.refs_0_), channel_id=1, source_target_pairs={{0,1},{1,0},{2,3},{3,2},{4,5},{5,4},{6,7},{7,6},{8,9},{9,8},{10,11... | collective-permute-start | bytes 7077896 | tf_op jit(solution)/shard_map/ppermute | solution.py:53
  271.4 488.8 %collective-permute-start.19 = (bf16[16,4,24,768]{3,2,0,1:T(8,128)(2,1)}, bf16[16,4,24,768]{3,2,0,1:T(8,128)(2,1)}, u32[]{:S(2)}, u32[]{:S(2)}) collective-permute-start(bf16[16,4,24,768]{3,2,0,1:T(8,128)(2,1)} %constant_dynamic-update-slice_fusion.15), channel_id=1, source_target_pairs={{0,1},{1,0},{2,3},{3,2},{4,5},{5,4},{6,7},{7,6},{8,9},{9,8},{10,11... | collective-permute-start | bytes 7077896 | tf_op jit(solution)/shard_map/ppermute | solution.py:53
  284.0 810.5 %collective-permute-start.29 = (bf16[16,96,768]{2,1,0:T(8,128)(2,1)}, bf16[16,96,768]{2,1,0:T(8,128)(2,1)}, u32[]{:S(2)}, u32[]{:S(2)}) collective-permute-start(bf16[16,96,768]{2,1,0:T(8,128)(2,1)} %constant_dynamic-update-slice_fusion.21.refs_0_), channel_id=1, source_target_pairs={{0,1},{1,0},{2,3},{3,2},{4,5},{5,4},{6,7},{7,6},{8,9},{9,8},{10,11... | collective-permute-start | bytes 7077896 | tf_op jit(solution)/shard_map/ppermute | solution.py:53
  285.1 655.4 %collective-permute-start.24 = (bf16[16,24,3072]{2,1,0:T(8,128)(2,1)}, bf16[16,24,3072]{2,1,0:T(8,128)(2,1)}, u32[]{:S(2)}, u32[]{:S(2)}) collective-permute-start(bf16[16,24,3072]{2,1,0:T(8,128)(2,1)} %constant_dynamic-update-slice_fusion.18.refs_0_), channel_id=1, source_target_pairs={{0,1},{1,0},{2,3},{3,2},{4,5},{5,4},{6,7},{7,6},{8,9},{9,8},{10,11... | collective-permute-start | bytes 7077896 | tf_op jit(solution)/shard_map/ppermute | solution.py:53
  1500.4 784.2 %collective-permute-start.32 = (bf16[16,24,3072]{2,1,0:T(8,128)(2,1)}, bf16[16,24,3072]{2,1,0:T(8,128)(2,1)}, u32[]{:S(2)}, u32[]{:S(2)}) collective-permute-start(bf16[16,24,3072]{2,1,0:T(8,128)(2,1)} %slice.602), channel_id=1, source_target_pairs={{0,1},{1,0},{2,3},{3,2},{4,5},{5,4},{6,7},{7,6},{8,9},{9,8},{10,11... | collective-permute-start | bytes 7077896 | tf_op jit(solution)/shard_map/ppermute | solution.py:53
  1648.6 647.8 %collective-permute-start.31 = (bf16[16,96,768]{2,1,0:T(8,128)(2,1)}, bf16[16,96,768]{2,1,0:T(8,128)(2,1)}, u32[]{:S(2)}, u32[]{:S(2)}) collective-permute-start(bf16[16,96,768]{2,1,0:T(8,128)(2,1)} %slice.600), channel_id=1, source_target_pairs={{0,1},{1,0},{2,3},{3,2},{4,5},{5,4},{6,7},{7,6},{8,9},{9,8},{10,11... | collective-permute-start | bytes 7077896 | tf_op jit(solution)/shard_map/ppermute | solution.py:53
  1797.4 491.5 %collective-permute-start.46 = (bf16[16,96,768]{2,1,0:T(8,128)(2,1)}, bf16[16,96,768]{2,1,0:T(8,128)(2,1)}, u32[]{:S(2)}, u32[]{:S(2)}) collective-permute-start(bf16[16,96,768]{2,1,0:T(8,128)(2,1)} %slice.621), channel_id=1, source_target_pairs={{0,1},{1,0},{2,3},{3,2},{4,5},{5,4},{6,7},{7,6},{8,9},{9,8},{10,11... | collective-permute-start | bytes 7077896 | tf_op jit(solution)/shard_map/ppermute | solution.py:53
  1945.6 348.0 %collective-permute-start.55 = (bf16[16,24,3072]{2,1,0:T(8,128)(2,1)}, bf16[16,24,3072]{2,1,0:T(8,128)(2,1)}, u32[]{:S(2)}, u32[]{:S(2)}) collective-permute-start(bf16[16,24,3072]{2,1,0:T(8,128)(2,1)} %slice.646), channel_id=1, source_target_pairs={{0,1},{1,0},{2,3},{3,2},{4,5},{5,4},{6,7},{7,6},{8,9},{9,8},{10,11... | collective-permute-start | bytes 7077896 | tf_op jit(solution)/shard_map/ppermute | solution.py:53
  2103.5 202.2 %collective-permute-start.45 = (bf16[16,96,768]{2,1,0:T(8,128)(2,1)}, bf16[16,96,768]{2,1,0:T(8,128)(2,1)}, u32[]{:S(2)}, u32[]{:S(2)}) collective-permute-start(bf16[16,96,768]{2,1,0:T(8,128)(2,1)} %slice.619), channel_id=1, source_target_pairs={{0,1},{1,0},{2,3},{3,2},{4,5},{5,4},{6,7},{7,6},{8,9},{9,8},{10,11... | collective-permute-start | bytes 7077896 | tf_op jit(solution)/shard_map/ppermute | solution.py:53
  2284.6 40.2 %collective-permute-start.30 = (bf16[16,96,768]{2,1,0:T(8,128)(2,1)S(1)}, bf16[16,96,768]{2,1,0:T(8,128)(2,1)S(1)}, u32[]{:S(2)}, u32[]{:S(2)}) collective-permute-start(bf16[16,96,768]{2,1,0:T(8,128)(2,1)S(1)} %slice.598), channel_id=1, source_target_pairs={{0,1},{1,0},{2,3},{3,2},{4,5},{5,4},{6,7},{7,6},{8,9},{9,8},{10,11... | collective-permute-start | bytes 7077896 | tf_op jit(solution)/shard_map/ppermute | solution.py:53
  2293.6 30.5 %collective-permute-start.47 = (bf16[8,96,768]{2,1,0:T(8,128)(2,1)S(1)}, bf16[8,96,768]{2,1,0:T(8,128)(2,1)S(1)}, u32[]{:S(2)}, u32[]{:S(2)}) collective-permute-start(bf16[8,96,768]{2,1,0:T(8,128)(2,1)S(1)} %slice.623), channel_id=1, source_target_pairs={{0,4},{1,3},{2,6},{3,1},{4,0},{5,7},{6,2},{7,5},{8,12},{9,11},{10,... | collective-permute-start | bytes 3538952 | tf_op jit(solution)/shard_map/ppermute | solution.py:53
  2325.6 27.9 %collective-permute-start.35 = (bf16[8,96,768]{2,1,0:T(8,128)(2,1)S(1)}, bf16[8,96,768]{2,1,0:T(8,128)(2,1)S(1)}, u32[]{:S(2)}, u32[]{:S(2)}) collective-permute-start(bf16[8,96,768]{2,1,0:T(8,128)(2,1)S(1)} %slice.487), channel_id=1, source_target_pairs={{0,4},{1,3},{2,6},{3,1},{4,0},{5,7},{6,2},{7,5},{8,12},{9,11},{10,... | collective-permute-start | bytes 3538952 | tf_op jit(solution)/shard_map/ppermute | solution.py:53
  2373.2 30.7 %collective-permute-start.37 = (bf16[8,96,768]{2,1,0:T(8,128)(2,1)S(1)}, bf16[8,96,768]{2,1,0:T(8,128)(2,1)S(1)}, u32[]{:S(2)}, u32[]{:S(2)}) collective-permute-start(bf16[8,96,768]{2,1,0:T(8,128)(2,1)S(1)} %slice.490), channel_id=1, source_target_pairs={{0,4},{1,3},{2,6},{3,1},{4,0},{5,7},{6,2},{7,5},{8,12},{9,11},{10,... | collective-permute-start | bytes 3538952 | tf_op jit(solution)/shard_map/ppermute | solution.py:53
  2377.2 27.2 %collective-permute-start.56 = (bf16[8,24,3072]{2,1,0:T(8,128)(2,1)S(1)}, bf16[8,24,3072]{2,1,0:T(8,128)(2,1)S(1)}, u32[]{:S(2)}, u32[]{:S(2)}) collective-permute-start(bf16[8,24,3072]{2,1,0:T(8,128)(2,1)S(1)} %slice.540), channel_id=1, source_target_pairs={{0,4},{1,3},{2,6},{3,1},{4,0},{5,7},{6,2},{7,5},{8,12},{9,11},{10,... | collective-permute-start | bytes 3538952 | tf_op jit(solution)/shard_map/ppermute | solution.py:53
  (153 other events, 3308.2 us)
Sparse Core Ops, SparseCore 0:
  2106.0 118.4 all-reduce.2

commit v2 on v1

v2 whole, which is shorter than its diff:
```python
import functools
import math

import jax
import jax.numpy as jnp
from jax import lax
from jax.experimental import pallas as pl
from jax.experimental.pallas import tpu as pltpu
from jax.sharding import PartitionSpec as P

HEADS = 12
HEAD_DIM = 64
REGIONS = 100

epsilon = 1e-12
F32 = jnp.float32
BF16 = jnp.bfloat16


def dense(left, right):
    return jnp.dot(left, right, preferred_element_type=F32)


def outer(left, right):
    return lax.dot_general(left, right, (((0,), (0,)), ((), ())), preferred_element_type=F32)


def back_dense(left, right):
    return lax.dot_general(left, right, (((1,), (1,)), ((), ())), preferred_element_type=F32)


def column_sum(values):
    return jnp.sum(values.astype(F32), axis=0)


def slot_valid(region_count, text_mask):
    region_slot = jnp.arange(REGIONS, dtype=jnp.int32)[None, :] < region_count[:, None]
    return jnp.concatenate([text_mask.astype(F32), region_slot.astype(F32)], axis=1)


def norm(values, gain, shift):
    center = values - jnp.mean(values, axis=-1, keepdims=True)
    spread = jnp.mean(center * center, axis=-1, keepdims=True)
    scale = lax.rsqrt(spread + epsilon)
    unit = center * scale
    return unit * gain + shift, (unit, scale)


def norm_back(saved, gain, grad):
    unit, scale = saved
    inner = grad * gain
    into = scale * (
        inner
        - jnp.mean(inner, axis=-1, keepdims=True)
        - unit * jnp.mean(inner * unit, axis=-1, keepdims=True)
    )
    return into, column_sum(grad * unit), column_sum(grad)


def forward_layer(inputs, weights, vectors, valid_keys):
    q_weight, k_weight, v_weight, o_weight, up_weight, down_weight = weights
    q_bias, v_bias, o_bias, gain_one, shift_one, up_bias, down_bias, gain_two, shift_two = vectors
    item_count = valid_keys.shape[0]
    row_count, width = inputs.shape

    def heads_of(values):
        return values.reshape(item_count, row_count // item_count, HEADS, HEAD_DIM)

    queries = heads_of((dense(inputs, q_weight) + q_bias).astype(BF16))
    key_rows = heads_of(dense(inputs, k_weight).astype(BF16))
    value_rows = heads_of((dense(inputs, v_weight) + v_bias).astype(BF16))
    scores = (
        jnp.einsum("bqhd,bkhd->bhqk", queries, key_rows, preferred_element_type=F32) * 0.125
    )
    scores = scores + (valid_keys[:, None, None, :] - 1.0) * 10000.0
    attention = jax.nn.softmax(scores, axis=-1)
    attention_low = attention.astype(BF16)
    context = jnp.einsum("bhqk,bkhd->bqhd", attention_low, value_rows, preferred_element_type=F32)
    context = context.astype(BF16).reshape(row_count, width)
    first_sum = inputs.astype(F32) + dense(context, o_weight) + o_bias
    middle, norm_one = norm(first_sum, gain_one, shift_one)
    middle = middle.astype(BF16)
    lifted = dense(middle, up_weight) + up_bias
    half = 0.5 * lax.erf(lifted * math.sqrt(0.5)) + 0.5
    activated = (lifted * half).astype(BF16)
    slope = half + lifted * jnp.exp(-0.5 * lifted * lifted) * (1.0 / math.sqrt(2.0 * math.pi))
    slope = slope.astype(BF16)
    second_sum = middle.astype(F32) + dense(activated, down_weight) + down_bias
    output, norm_two = norm(second_sum, gain_two, shift_two)
    saved = (queries, key_rows, value_rows, attention, attention_low, context, norm_one, middle, slope, activated, norm_two)
    return output.astype(BF16), saved


def backward_layer(inputs, weights, vectors, saved, out_grad, send):
    q_weight, k_weight, v_weight, o_weight, up_weight, down_weight = weights
    q_bias, v_bias, o_bias, gain_one, shift_one, up_bias, down_bias, gain_two, shift_two = vectors
    queries, key_rows, value_rows, attention, attention_low, context, norm_one, middle, slope, activated, norm_two = saved
    row_count, width = inputs.shape
    sum_grad, gain_two_grad, shift_two_grad = norm_back(norm_two, gain_two, out_grad)
    lowered_grad = sum_grad.astype(BF16)
    send("down", [outer(activated, lowered_grad)])
    lifted_grad = (back_dense(lowered_grad, down_weight) * slope).astype(BF16)
    send("up", [outer(middle, lifted_grad)])
    middle_grad = sum_grad + back_dense(lifted_grad, up_weight)
    first_grad, gain_one_grad, shift_one_grad = norm_back(norm_one, gain_one, middle_grad)
    attended_grad = first_grad.astype(BF16)
    o_grad = outer(context, attended_grad)
    context_grad = back_dense(attended_grad, o_weight).astype(BF16).reshape(queries.shape)
    attention_grad = jnp.einsum(
        "bqhd,bkhd->bhqk", context_grad, value_rows, preferred_element_type=F32
    )
    value_grad = jnp.einsum(
        "bhqk,bqhd->bkhd", attention_low, context_grad, preferred_element_type=F32
    )
    value_grad = value_grad.astype(BF16).reshape(row_count, width)
    weighed = attention * attention_grad
    score_grad = (weighed - attention * jnp.sum(weighed, axis=-1, keepdims=True)).astype(BF16)
    query_grad = (
        jnp.einsum("bhqk,bkhd->bqhd", score_grad, key_rows, preferred_element_type=F32) * 0.125
    )
    query_grad = query_grad.astype(BF16).reshape(row_count, width)
    key_grad = (
        jnp.einsum("bhqk,bqhd->bkhd", score_grad, queries, preferred_element_type=F32) * 0.125
    )
    key_grad = key_grad.astype(BF16).reshape(row_count, width)
    send("four", [outer(inputs, query_grad), outer(inputs, key_grad), outer(inputs, value_grad), o_grad])
    input_grad = (
        first_grad
        + back_dense(query_grad, q_weight)
        + back_dense(key_grad, k_weight)
        + back_dense(value_grad, v_weight)
    )
    small = (column_sum(query_grad), column_sum(value_grad), column_sum(attended_grad), gain_one_grad, shift_one_grad, column_sum(lifted_grad), column_sum(lowered_grad), gain_two_grad, shift_two_grad)
    return input_grad, small


def plain(weights, small, valid_keys, hidden, cotangent):
    owners = lax.axis_size("dp")
    layers = weights[0].shape[0]
    packed = jnp.concatenate([v.reshape(1, -1) for v in small], axis=1)
    packed = lax.all_gather(packed, "dp", axis=0, tiled=True).astype(F32)
    vectors = []
    offset = 0
    for v in small:
        size = v.shape[0] * v.shape[1]
        part = packed[:, offset : offset + size].reshape((owners,) + v.shape)
        vectors.append(jnp.swapaxes(part, 0, 1).reshape(layers, -1))
        offset += size
    vectors = [tuple(v[layer] for v in vectors) for layer in range(layers)]
    gathered = [
        tuple(lax.all_gather(w[layer], "dp", axis=0, tiled=True) for w in weights)
        for layer in range(layers)
    ]
    current = hidden
    inputs, saved = [], []
    for layer in range(layers):
        inputs.append(current)
        current, kept = forward_layer(current, gathered[layer], vectors[layer], valid_keys)
        saved.append(kept)
    flowing = cotangent.astype(F32)
    big = [{} for _ in range(layers)]
    tiny = [None] * layers
    for layer in reversed(range(layers)):

        def send(name, grads, layer=layer):
            big[layer][name] = [
                lax.psum_scatter(g.astype(BF16).reshape(owners, -1, g.shape[-1]), "dp", scatter_dimension=0, tiled=True)[0].astype(F32)
                for g in grads
            ]

        flowing, tiny[layer] = backward_layer(
            inputs[layer], gathered[layer], vectors[layer], saved[layer], flowing, send
        )
    flat = jnp.concatenate(
        [g.reshape(owners, -1) for layer in range(layers) for g in tiny[layer]], axis=1
    )
    flat = lax.psum_scatter(flat, "dp", scatter_dimension=0, tiled=True).reshape(layers, -1)
    summed = []
    offset = 0
    for v in small:
        summed.append(flat[:, offset : offset + v.shape[1]])
        offset += v.shape[1]
    q_b, v_b, o_b, g_one, s_one, u_b, d_b, g_two, s_two = summed
    fours = [jnp.stack([big[layer]["four"][i] for layer in range(layers)]) for i in range(4)]
    up = jnp.stack([big[layer]["up"][0] for layer in range(layers)])
    down = jnp.stack([big[layer]["down"][0] for layer in range(layers)])
    return (
        current, flowing, *fours,
        q_b, v_b, o_b, g_one, s_one, up, u_b, down, d_b, g_two, s_two,
    )


ITEM = 256
PAD = -1e30


def table_of(owners):
    chips = owners // 2
    depth = chips // 4
    me = lax.axis_index("dp")
    chip, core = me // 2, me % 2
    walk = jnp.arange(chips, dtype=jnp.int32)

    def chip_at(position, core):
        z, first, second = position % depth, position // depth % 2, position // (2 * depth)
        return chip ^ (z * 4 + jnp.where(core == 0, second * 2 + first, first * 2 + second))

    def place_of(other, core):
        z, y, x = (other ^ chip) // 4, (other ^ chip) // 2 % 2, (other ^ chip) % 2
        return z + depth * jnp.where(core == 0, x + 2 * y, y + 2 * x)

    return jnp.concatenate(
        [chip_at(walk, core), chip_at(walk, 1 - core), place_of(walk, core), place_of(walk, 1 - core), core[None]]
    ).astype(jnp.int32)


def flip(value, owners, even, odd):
    return lax.ppermute(value, "dp", [(i, i ^ (odd if i % 2 else even)) for i in range(owners)])


MICROS = {
    "attend_forward": 18, "lift": 13, "lower": 9, "lower_back": 6, "lift_back": 15, "attend_back_first": 13,
    "attend_back_second": 10, "attend_back_third": 5, "attend_back_last": 6,
}


def padded_bytes(shape, dtype):
    *lead, rows, columns = (1,) * max(0, 2 - len(shape)) + tuple(shape)
    return math.prod(lead) * (-(-rows // 16) * 16) * (-(-columns // 128) * 128) * jnp.dtype(dtype).itemsize


def launch(body, outs, smem=(), vmem=(), hbm=(), deps=(), scratch=(), extra=3):
    counts = (len(smem), len(vmem), len(hbm), len(deps), len(outs))
    name = getattr(body, "func", body).__name__
    micros = MICROS.get(name, 2)
    held = [(v.shape, v.dtype) for v in vmem] + list(outs)
    held += [(v.shape, v.dtype) for v in scratch if jnp.issubdtype(v.dtype, jnp.floating)]
    limit = extra * 2**20 + sum(padded_bytes(shape, dtype) for shape, dtype in held)

    def kernel(*refs):
        groups, at = [], 0
        for count in counts:
            groups.append(refs[at : at + count])
            at += count
        body(groups[0], groups[1], groups[2], groups[4], refs[at:])

    in_specs = (
        [pl.BlockSpec(memory_space=pltpu.SMEM)] * len(smem)
        + [pl.BlockSpec(memory_space=pltpu.VMEM)] * len(vmem)
        + [pl.BlockSpec(memory_space=pl.ANY)] * (len(hbm) + len(deps))
    )
    return pl.pallas_call(
        kernel,
        out_shape=[jax.ShapeDtypeStruct(s, d) for s, d in outs],
        in_specs=in_specs,
        out_specs=[pl.BlockSpec(memory_space=pltpu.VMEM)] * len(outs),
        scratch_shapes=list(scratch),
        name=name,
        compiler_params=pltpu.CompilerParams(vmem_limit_bytes=limit),
        cost_estimate=pl.CostEstimate(
            flops=int(micros * 1e9), bytes_accessed=int(micros * 3e6), transcendentals=0
        ),
    )(*smem, *vmem, *hbm, *deps)


def mm(left, right):
    return jnp.dot(left, right, preferred_element_type=F32)


def mm_nt(left, right):
    return lax.dot_general(left, right, (((1,), (1,)), ((), ())), preferred_element_type=F32)


def mm_tn(left, right):
    return lax.dot_general(left, right, (((0,), (0,)), ((), ())), preferred_element_type=F32)


def fetch(tab, parts, whole, sems, columns=None):
    near, near_more, far, far_more = parts
    half, rows = near.shape[0], near.shape[1]
    core = tab[8 * half]
    start, stop = (0, near.shape[2]) if columns is None else columns
    step = (stop - start) // 3 if (stop - start) % 384 == 0 and rows > 128 else (768 if (stop - start) % 768 == 0 else 384)
    copies = []
    for side, group in enumerate(((near, near_more), (far, far_more))):
        hand = core if side == 0 else 1 - core
        for which, part in enumerate(group):
            for b in range(half):
                chip = tab[(2 * side + which) * half + b]
                for at in range(start, stop, step):
                    source = part.at[b, :, pl.ds(at, step)]
                    to = pl.ds(pl.multiple_of(chip * rows, 16), rows)
                    target = whole.at[hand, to, pl.ds(at - start, step)]
                    copies.append(pltpu.make_async_copy(source, target, sems.at[len(copies)]))
                    copies[-1].start()
    return copies


def fetch_packed(tab, parts, kind, whole, sems, columns=None):
    near, far = parts
    chips, rows = near.shape[0], near.shape[1] // 3
    core = tab[4 * chips]
    copies = []

    def move(source, target):
        copies.append(pltpu.make_async_copy(source, target, sems.at[len(copies)]))
        copies[-1].start()

    for part, hand in ((near, core), (far, 1 - core)):
        for chip in range(chips):
            if kind == "down":
                wide = whole.shape[2]
                for g in range(4):
                    source = part.at[chip, pl.ds(2 * rows, rows), pl.ds(g * wide, wide)]
                    move(source, whole.at[hand, pl.ds((4 * chip + g) * rows, rows)])
                continue
            at = pl.ds(0 if kind == "four" else rows, rows)
            start, stop = (0, whole.shape[2]) if columns is None else columns
            step = (768 if (stop - start) % 768 == 0 else 384)
            for c in range(start, stop, step):
                source = part.at[chip, at, pl.ds(c, step)]
                move(source, whole.at[hand, pl.ds(chip * rows, rows), pl.ds(c - start, step)])
    return copies


def bring(tab, parts, kind, whole, sems, columns=None):
    if len(parts) == 2:
        return fetch_packed(tab, parts, kind, whole, sems, columns)
    return fetch(tab, parts, whole, sems, columns)


def finish(copies):
    for copy in copies:
        copy.wait()


def norm_rows(values):
    center = values - jnp.mean(values, axis=-1, keepdims=True)
    scale = lax.rsqrt(jnp.mean(center * center, axis=-1, keepdims=True) + epsilon)
    return center * scale, scale


def norm_rows_back(unit, scale, inner):
    return scale * (
        inner
        - jnp.mean(inner, axis=-1, keepdims=True)
        - unit * jnp.mean(inner * unit, axis=-1, keepdims=True)
    )


def gelu_and_slope(v):
    z = jnp.abs(v) * math.sqrt(0.5)
    t = 1.0 / (1.0 + 0.3275911 * z)
    bell = jnp.exp(-0.5 * v * v)
    poly = 0.5 * 1.061405429 * t - 0.5 * 1.453152027
    poly = poly * t + 0.5 * 1.421413741
    poly = poly * t - 0.5 * 0.284496736
    poly = poly * t + 0.5 * 0.254829592
    tail = poly * t * bell
    phi = jnp.where(v >= 0.0, 1.0 - tail, tail)
    return v * phi, phi + v * bell * (1.0 / math.sqrt(2.0 * math.pi))


Q_B, V_B, O_B, G_ONE, S_ONE, D_B, G_TWO, S_TWO, UP_B = range(9)


def split_own(smem, vmem, hbm, outs, scratch):
    (tab,) = smem
    core = tab[tab.shape[0] - 1]
    q, k, v, o, up, down = vmem
    layers = q.shape[0]
    for layer in range(layers):
        for place, hand in ((0, core), (1, 1 - core)):
            four, wide, tall = outs[6 * layer + 3 * place : 6 * layer + 3 * place + 3]
            part = q.shape[2] // 2
            at = pl.ds(pl.multiple_of(hand * part, 128), part)
            for i, w in enumerate((q, k, v, o)):
                four[:, i * part : (i + 1) * part] = w[layer, :, at]
            part = up.shape[2] // 2
            wide[...] = up[layer, :, pl.ds(pl.multiple_of(hand * part, 128), part)]
            part = down.shape[2] // 2
            tall[...] = down[layer, :, pl.ds(pl.multiple_of(hand * part, 128), part)]


def join_rows(smem, vmem, hbm, outs, scratch):
    (tab,) = smem
    first = tab[tab.shape[0] - 1] == 0
    for i, out in enumerate(outs):
        mine, came = vmem[2 * i][...].astype(F32), vmem[2 * i + 1][...].astype(F32)
        rows = mine.shape[0]
        upper = jnp.where(first, mine, came)
        lower = jnp.where(first, came, mine)
        out[...] = jnp.concatenate([upper, lower], axis=0).astype(out.dtype)


def join_blocks(smem, vmem, hbm, outs, scratch):
    (out,) = outs
    (sems,) = scratch
    at = 0
    copies = []
    for part in hbm:
        count = part.shape[0] if len(part.shape) == 3 else 1
        target = out.at[pl.ds(at, count)] if len(part.shape) == 3 else out.at[at]
        copies.append(pltpu.make_async_copy(part, target, sems.at[len(copies)]))
        copies[-1].start()
        at += count
    finish(copies)


def attend_forward(smem, vmem, hbm, outs, scratch):
    (tab,) = smem
    x, vec, mask = vmem
    q, k, v, p, context, unit, scale, middle = outs
    whole, sems = scratch
    finish(bring(tab, hbm, "four", whole, sems))
    half = x.shape[1] // 2
    for h in (0, 1):
        at = slice(h * half, (h + 1) * half)
        made = mm(x[...], whole[h, :, 0 : 3 * half])
        q[:, at] = (made[:, 0:half] + vec[Q_B : Q_B + 1, at]).astype(BF16)
        k[:, at] = made[:, half : 2 * half].astype(BF16)
        v[:, at] = (made[:, 2 * half :] + vec[V_B : V_B + 1, at]).astype(BF16)
    low = lax.broadcasted_iota(jnp.int32, (ITEM, 2 * HEAD_DIM), 1) < HEAD_DIM
    items = x.shape[0] // ITEM

    def pair(i, carry):
        at = pl.ds(pl.multiple_of(i * 2 * HEAD_DIM, 2 * HEAD_DIM), 2 * HEAD_DIM)
        for item in range(items):
            rows = slice(item * ITEM, (item + 1) * ITEM)
            qs, ks, vs = q[rows, at], k[rows, at], v[rows, at]
            made = []
            for side in (0, 1):
                own = low if side == 0 else jnp.logical_not(low)
                s = mm_nt(jnp.where(own, qs, jnp.zeros_like(qs)), ks) * 0.125 + mask[item]
                e = jnp.exp(s - jnp.max(s, axis=-1, keepdims=True))
                w = (e * (1.0 / jnp.sum(e, axis=-1, keepdims=True))).astype(BF16)
                p[item * HEADS + 2 * i + side] = w
                made.append(mm(w, vs))
            context[rows, at] = jnp.where(low, made[0], made[1]).astype(BF16)
        return carry

    lax.fori_loop(0, HEADS // 2, pair, 0)
    attended = jnp.concatenate([mm(context[...], whole[h, :, 3 * half :]) for h in (0, 1)], axis=1)
    first = x[...].astype(F32) + (attended + vec[O_B : O_B + 1, :])
    made, made_scale = norm_rows(first)
    unit[...] = made
    scale[...] = made_scale
    middle[...] = (made * vec[G_ONE : G_ONE + 1, :] + vec[S_ONE : S_ONE + 1, :]).astype(BF16)


def lift(smem, vmem, hbm, outs, scratch):
    (tab,) = smem
    middle, vec = vmem
    activated, slope = outs
    whole, sems = scratch
    finish(bring(tab, hbm, "up", whole, sems))
    half = whole.shape[2]
    width = vec.shape[1]
    step = width // 2
    for h in (0, 1):
        for j in range(half // step):
            at = slice(j * step, (j + 1) * step)
            column = h * half + j * step
            bias = vec[UP_B + column // width : UP_B + column // width + 1, column % width : column % width + step]
            a, s = gelu_and_slope(mm(middle[...], whole[h, :, at]) + bias)
            activated[h, :, at] = a.astype(BF16)
            slope[h, :, at] = s.astype(BF16)


def lower(smem, vmem, hbm, outs, scratch):
    (tab,) = smem
    activated, middle, vec = vmem
    output, unit, scale = outs
    whole, sems = scratch
    finish(bring(tab, hbm, "down", whole, sems))
    deep = activated.shape[2]
    lowered = jnp.concatenate(
        [
            mm(activated[0], whole[h, 0:deep, :]) + mm(activated[1], whole[h, deep:, :])
            for h in (0, 1)
        ],
        axis=1,
    )
    second = middle[...].astype(F32) + (lowered + vec[D_B : D_B + 1, :])
    made, made_scale = norm_rows(second)
    unit[...] = made
    scale[...] = made_scale
    output[...] = (made * vec[G_TWO : G_TWO + 1, :] + vec[S_TWO : S_TWO + 1, :]).astype(BF16)


def rows_sum(values):
    return jnp.sum(values, axis=0, keepdims=True)


def place_in(tab, places, chips, chip, ordered):
    return chip if ordered else tab[places * chips + chip]


def lower_back(smem, vmem, hbm, outs, scratch, ordered=False):
    (tab,) = smem
    grad, unit, scale, vec, activated = vmem
    sum_grad, lowered_grad, send, keep, sums = outs
    chips, rows, part = send.shape
    core = tab[4 * chips]
    g = grad[...].astype(F32)
    u = unit[...]
    made = norm_rows_back(u, scale[...], g * vec[G_TWO : G_TWO + 1, :])
    sum_grad[...] = made
    low = made.astype(BF16)
    half = low.shape[1] // 2
    lowered_grad[0] = low[:, :half]
    lowered_grad[1] = low[:, half:]
    sums[...] = jnp.zeros_like(sums)
    sums[0:1, :] = rows_sum(g * u)
    sums[1:2, :] = rows_sum(g)
    sums[2:3, :] = rows_sum(low.astype(F32))
    deep = activated.shape[2]
    wide = part // 4
    for out, hand, places in ((send, 1 - core, 3), (keep, core, 2)):
        right = lowered_grad[hand]
        for h in (0, 1):
            for j in range(deep // (8 * rows)):
                made = mm_tn(activated[h, :, 8 * rows * j : 8 * rows * (j + 1)], right).astype(BF16)
                for i in (0, 1):
                    chip = h * deep // (4 * rows) + 2 * j + i
                    to = place_in(tab, places, chips, chip, ordered)
                    for g in range(4):
                        at = (4 * i + g) * rows
                        out[to, :, g * wide : (g + 1) * wide] = made[at : at + rows]


def lift_back(smem, vmem, hbm, outs, scratch, ordered=False):
    (tab,) = smem
    lowered_grad, slope, middle = vmem
    lifted_grad, send, keep, sums = outs
    whole, sems, turned = scratch
    copies = bring(tab, hbm, "down", whole, sems)
    chips, rows, part = send.shape
    core = tab[4 * chips]
    turned[...] = middle[...].T
    finish(copies)
    width = sums.shape[1]
    step = width // 2
    sums[...] = jnp.zeros_like(sums)
    for h in (0, 1):
        for j in range(part // step):
            at = slice(j * step, (j + 1) * step)
            deep = slice(h * part + j * step, h * part + (j + 1) * step)
            made = mm_nt(lowered_grad[0], whole[0, deep, :]) + mm_nt(lowered_grad[1], whole[1, deep, :])
            made = (made * slope[h, :, at].astype(F32)).astype(BF16)
            lifted_grad[h, :, at] = made
            column = h * part + j * step
            sums[column // width : column // width + 1, column % width : column % width + step] = rows_sum(made.astype(F32))
    for out, hand, places in ((send, 1 - core, 3), (keep, core, 2)):
        for j in range(part // step):
            at = slice(j * step, (j + 1) * step)
            made = mm(turned[...], lifted_grad[hand, :, at]).astype(BF16)
            for chip in range(chips):
                out[place_in(tab, places, chips, chip, ordered), :, at] = made[chip * rows : (chip + 1) * rows]


def attend_back_first(smem, vmem, hbm, outs, scratch):
    (tab,) = smem
    sum_grad, lifted_grad, unit, scale, vec = vmem
    first_grad, attended_grad, context_grad, sums = outs
    whole, sems, o_whole, o_sems = scratch
    half = o_whole.shape[2]
    up_parts, four_parts = hbm[: len(hbm) // 2], hbm[len(hbm) // 2 :]
    copies = bring(tab, up_parts, "up", whole, sems)
    o_copies = bring(tab, four_parts, "four", o_whole, o_sems, columns=(3 * half, 4 * half))
    finish(copies)
    grad = sum_grad[...] + mm_nt(lifted_grad[0], whole[0]) + mm_nt(lifted_grad[1], whole[1])
    u = unit[...]
    made = norm_rows_back(u, scale[...], grad * vec[G_ONE : G_ONE + 1, :])
    first_grad[...] = made
    low = made.astype(BF16)
    attended_grad[0] = low[:, :half]
    attended_grad[1] = low[:, half:]
    sums[...] = jnp.zeros_like(sums)
    sums[0:1, :] = rows_sum(grad * u)
    sums[1:2, :] = rows_sum(grad)
    sums[2:3, :] = rows_sum(low.astype(F32))
    finish(o_copies)
    context_grad[...] = (mm_nt(low[:, :half], o_whole[0]) + mm_nt(low[:, half:], o_whole[1])).astype(BF16)


def attend_back_second(smem, vmem, hbm, outs, scratch):
    q, k, v, p, context_grad, attended_grad = vmem
    (grads,) = outs
    half = attended_grad.shape[2]
    items = q.shape[0] // ITEM
    low = lax.broadcasted_iota(jnp.int32, (ITEM, 2 * HEAD_DIM), 1) < HEAD_DIM
    pairs = HEADS // 4
    for h in (0, 1):
        grads[h, :, 3 * half :] = attended_grad[h]

        def pair(i, carry, h=h):
            at = pl.ds(pl.multiple_of(h * half + i * 2 * HEAD_DIM, 2 * HEAD_DIM), 2 * HEAD_DIM)
            for item in range(items):
                rows = slice(item * ITEM, (item + 1) * ITEM)
                qs, ks, vs, cs = q[rows, at], k[rows, at], v[rows, at], context_grad[rows, at]
                made = []
                for side in (0, 1):
                    own = low if side == 0 else jnp.logical_not(low)
                    w = p[item * HEADS + 2 * (h * pairs + i) + side]
                    wide = w.astype(F32)
                    g = mm_nt(jnp.where(own, cs, jnp.zeros_like(cs)), vs)
                    g = wide * g
                    d = (g - wide * jnp.sum(g, axis=-1, keepdims=True)).astype(BF16)
                    made.append((mm(d, ks), mm_tn(d, qs), mm_tn(w, cs)))
                for place, scale in ((0, 0.125), (1, 0.125), (2, 1.0)):
                    both = jnp.where(low, made[0][place], made[1][place]) * scale
                    to = pl.ds(pl.multiple_of(place * half + i * 2 * HEAD_DIM, 2 * HEAD_DIM), 2 * HEAD_DIM)
                    grads[h, rows, to] = both.astype(BF16)
            return carry

        lax.fori_loop(0, pairs, pair, 0)


def attend_back_third(smem, vmem, hbm, outs, scratch, ordered=False):
    (tab,) = smem
    x, context, grads = vmem
    send, keep, sums = outs
    x_turned, c_turned = scratch
    chips, rows, part = send.shape
    half = part // 4
    core = tab[4 * chips]
    x_turned[...] = x[...].T
    c_turned[...] = context[...].T
    for out, hand, places in ((send, 1 - core, 3), (keep, core, 2)):
        for j in range(4):
            at = slice(j * half, (j + 1) * half)
            made = mm((c_turned if j == 3 else x_turned)[...], grads[hand, :, at]).astype(BF16)
            for chip in range(chips):
                out[place_in(tab, places, chips, chip, ordered), :, at] = made[chip * rows : (chip + 1) * rows]
    sums[...] = jnp.zeros_like(sums)
    for h in (0, 1):
        at = slice(h * half, (h + 1) * half)
        sums[0:1, at] = rows_sum(grads[h, :, 0:half].astype(F32))
        sums[1:2, at] = rows_sum(grads[h, :, 2 * half : 3 * half].astype(F32))


def attend_back_last(smem, vmem, hbm, outs, scratch):
    (tab,) = smem
    first_grad, grads = vmem
    (out,) = outs
    whole, sems = scratch
    deep = whole.shape[2]
    finish(bring(tab, hbm, "four", whole, sems, columns=(0, deep)))
    out[...] = first_grad[...] + mm_nt(grads[0, :, :deep], whole[0]) + mm_nt(grads[1, :, :deep], whole[1])


def add_halves(smem, vmem, hbm, outs, scratch):
    keep, came = vmem
    send, kept = outs
    half = send.shape[0]

    def block(b, carry):
        kept[b] = (keep[b].astype(F32) + came[b].astype(F32)).astype(BF16)
        send[b] = (keep[half + b].astype(F32) + came[half + b].astype(F32)).astype(BF16)
        return carry

    lax.fori_loop(0, half, block, 0)


def add_spread(smem, vmem, hbm, outs, scratch):
    keep, came = vmem
    for b, out in enumerate(outs):
        out[...] = (keep[b].astype(F32) + came[b].astype(F32)).astype(out.dtype)


def add_packed(smem, vmem, hbm, outs, scratch):
    (out,) = outs
    rows = vmem[0].shape[1]

    def block(b, carry):
        for i in range(len(vmem) // 2):
            both = vmem[2 * i][b].astype(F32) + vmem[2 * i + 1][b].astype(F32)
            out[b, i * rows : (i + 1) * rows] = both.astype(BF16)
        return carry

    lax.fori_loop(0, out.shape[0], block, 0)


def add_last(smem, vmem, hbm, outs, scratch, kinds=()):
    (tab,) = smem
    core = tab[tab.shape[0] - 1]
    (total,) = scratch
    made = vmem[0][...].astype(F32)
    for came in vmem[1:]:
        made = made + came[...].astype(F32)
    total[...] = made
    rows = total.shape[0] // len(kinds)
    for i, kind in enumerate(kinds):
        for out, hand in ((outs[2 * i], core), (outs[2 * i + 1], 1 - core)):
            if kind == "down":
                wide = total.shape[1] // 2
                out[...] = total[i * rows : (i + 1) * rows, pl.ds(pl.multiple_of(hand * wide, 128), wide)]
            else:
                half = rows // 2
                out[...] = total[pl.ds(pl.multiple_of(i * rows + hand * half, 8), half), :]


def write_out(smem, vmem, hbm, outs, scratch, kind=""):
    (tab,) = smem
    core = tab[tab.shape[0] - 1]
    half = outs[0].shape[2] // 2
    for layer in range(len(vmem) // 2):
        for hand, part in ((core, vmem[2 * layer]), (1 - core, vmem[2 * layer + 1])):
            at = pl.ds(pl.multiple_of(hand * half, 128), half)
            if kind == "down":
                rows = part.shape[0]
                for g in (0, 1):
                    outs[0][layer, g * rows : (g + 1) * rows, at] = part[:, g * half : (g + 1) * half]
                continue
            for i, out in enumerate(outs):
                out[layer, :, at] = part[:, i * half : (i + 1) * half]


def join_packed(smem, vmem, hbm, outs, scratch):
    (tab,) = smem
    first = tab[tab.shape[0] - 1] == 0
    (out,) = outs
    joined = []
    for i in range(3):
        mine, came = vmem[2 * i][...].astype(F32), vmem[2 * i + 1][...].astype(F32)
        joined.append([jnp.where(first, mine, came), jnp.where(first, came, mine)])
    rows = out.shape[0] // 3
    for i in (0, 1):
        out[i * rows : (i + 1) * rows] = jnp.concatenate(joined[i], axis=0).astype(BF16)
    wide = joined[2][0].shape[1]
    for g in range(4):
        part = joined[2][g // 2][g % 2 * rows : (g % 2 + 1) * rows]
        out[2 * rows :, g * wide : (g + 1) * wide] = part.astype(BF16)


def add_two(smem, vmem, hbm, outs, scratch):
    outs[0][...] = vmem[0][...] + vmem[1][...]


class Chain:
    def __init__(self):
        self.token = None

    def __call__(self, body, outs, after=(), **kinds):
        deps = list(after) + ([] if self.token is None else [self.token])
        made = launch(body, outs, deps=deps, **kinds)
        self.token = min(made, key=lambda m: m.size)
        return made


def spread_vectors(small, owners):
    me = lax.axis_index("dp")
    layers = small[0].shape[0]
    short = [v for v in small if v.shape[1] == small[0].shape[1]]
    (long,) = [v for v in small if v.shape[1] != small[0].shape[1]]
    width = short[0].shape[1] * owners
    lanes = jnp.arange(width, dtype=jnp.int32)

    def spread(values, start):
        count = values.shape[1]
        hit = lanes[None, :] == start + jnp.arange(count, dtype=jnp.int32)[:, None]
        return jnp.dot(values, hit.astype(BF16), preferred_element_type=F32)

    count = short[0].shape[1]
    plain = spread(jnp.stack(short, axis=1).reshape(-1, count), me * count)
    count = long.shape[1]
    rows = count * owners // width
    wide = spread(long, me * count % width)
    row = jnp.arange(rows, dtype=jnp.int32)[None, :, None] == me * count // width
    wide = jnp.where(row, wide[:, None, :], 0.0)
    own = jnp.concatenate([plain.reshape(layers, -1, width), wide], axis=1)
    return own.reshape(-1, width).astype(BF16)


def own_share(total, counts, owners):
    me = lax.axis_index("dp")
    layers, _, width = total.shape
    out = []
    row = 0
    for count in counts:
        rows = count * owners // width
        whole = total[:, row : row + rows].reshape(layers, -1)
        out.append(lax.dynamic_slice_in_dim(whole, me * count, count, axis=1))
        row += rows
    return out


def blocks(weights, small, mask, hidden, cotangent, seq):
    q_weight, k_weight, v_weight, o_weight, up_weight, down_weight = weights
    owners = lax.axis_size("dp")
    chips = owners // 2
    depth = chips // 4
    layers, rows, width = q_weight.shape
    wide = up_weight.shape[2]
    items = hidden.shape[0] // seq
    tall = items * ITEM
    tab = table_of(owners)
    chain = Chain()
    dma = lambda n: pltpu.SemaphoreType.DMA((n,))
    xy_one = lambda v: flip(v, owners, 2, 4)
    xy_two = lambda v: flip(v, owners, 4, 2)
    core_flip = lambda v: flip(v, owners, 1, 1)
    z_flip = lambda v, k: flip(v, owners, 8 * k, 8 * k)
    bits = [lambda v, b=b: flip(v, owners, 1 << b, 1 << b) for b in range(int(math.log2(owners)))]
    same_core = [list(range(core, owners, 2)) for core in (0, 1)]

    def padded(values):
        spread = values.reshape(items, seq, width)
        return jnp.pad(spread, ((0, 0), (0, ITEM - seq), (0, 0))).reshape(tall, width)

    x = padded(hidden)
    grad = padded(cotangent)

    block = (2 * rows, 2 * width)
    shape = {"four": block, "up": (2 * rows, wide // 2), "down": (2 * down_weight.shape[1], width // 2)}
    kinds = ("four", "up", "down")
    halves = [((shape[k][0] // 2, shape[k][1]), BF16) for k in kinds]
    split = chain(split_own, halves * 2 * layers, smem=[tab], vmem=list(weights))
    mine = lambda layer: split[6 * layer : 6 * layer + 3]
    other = [[core_flip(v) for v in split[6 * layer + 3 : 6 * layer + 6]] for layer in range(layers)]
    both = lambda layer: [v for two in zip(mine(layer), other[layer]) for v in two]
    own, near, far = {}, {}, {}
    z_came, x_one, x_two, stacked = {}, {}, {}, {}

    (pack,) = chain(join_packed, [((3 * block[0], block[1]), BF16)], smem=[tab], vmem=both(1))
    packed = lax.all_gather(pack, "dp", axis=0, tiled=True, axis_index_groups=same_core)
    made = chain(join_rows, [(shape[k], BF16) for k in kinds], smem=[tab], vmem=both(0))
    for kind, value in zip(kinds, made):
        own[kind] = value

    def z_round(kind):
        z_came[kind] = [z_flip(own[kind], k) for k in range(1, depth)]

    def first_stack(kind, after=()):
        r, c = shape[kind]
        (stacked[kind],) = chain(join_blocks, [((depth, r, c), BF16)], hbm=[own[kind]] + z_came[kind], scratch=[dma(depth)], after=after)
        x_one[kind] = xy_one(stacked[kind])

    def second_stack(kind, after=()):
        r, c = shape[kind]
        (made,) = chain(join_blocks, [((2 * depth, r, c), BF16)], hbm=[stacked[kind], x_one[kind]], scratch=[dma(2)], after=after)
        x_two[kind] = xy_two(made)
        near[kind] = [made, x_two[kind]]
        far[kind] = [core_flip(made)]

    def third(kind):
        far[kind].append(core_flip(x_two[kind]))

    vectors = spread_vectors(small, owners)

    def vector_round(bit):
        nonlocal vectors
        (vectors,) = chain(add_two, [(vectors.shape, vectors.dtype)], vmem=[vectors, bits[bit](vectors)])

    def land():
        nonlocal packed
        value = lax.optimization_barrier((packed, chain.token))[0].reshape((chips,) + pack.shape)
        packed = [value, core_flip(value)]

    parts = lambda layer, kind: near[kind] + far[kind] if layer == 0 else packed
    whole = lambda kind, columns=None: [pltpu.VMEM((2, shape[kind][0] * chips, columns or shape[kind][1]), BF16), dma(8 * chips)]
    xs, kept = [x], [{} for _ in range(layers)]
    row = lambda dtype: ((tall, width), dtype)
    column = ((tall, 1), F32)
    deep = ((2, tall, wide // 2), BF16)

    def forward_attend(layer):
        s = kept[layer]
        s["q"], s["k"], s["v"], s["p"], s["context"], s["unit_one"], s["scale_one"], s["middle"] = chain(
            attend_forward,
            [row(BF16)] * 3 + [((items * HEADS, ITEM, ITEM), BF16), row(BF16), row(F32), column, row(BF16)],
            smem=[tab], vmem=[xs[layer], vec[layer], mask], hbm=parts(layer, "four"), scratch=whole("four"),
        )

    def forward_lift(layer):
        s = kept[layer]
        s["activated"], s["slope"] = chain(
            lift, [deep, deep], smem=[tab], vmem=[s["middle"], vec[layer]], hbm=parts(layer, "up"), scratch=whole("up"),
        )

    def forward_lower(layer):
        s = kept[layer]
        output, s["unit_two"], s["scale_two"] = chain(
            lower, [row(BF16), row(F32), column], smem=[tab], vmem=[s["activated"], s["middle"], vec[layer]],
            hbm=parts(layer, "down"), scratch=whole("down"),
        )
        xs.append(output)

    z_round("four")
    z_round("up")
    vector_round(0)
    first_stack("four")
    vector_round(1)
    vector_round(2)
    second_stack("four")
    vector_round(3)
    z_round("down")
    first_stack("up")
    vector_round(4)
    vec = vectors.astype(F32).reshape(layers, -1, width)
    third("four")
    second_stack("up", after=[x_two["four"]])
    first_stack("down")
    forward_attend(0)
    third("up")
    second_stack("down", after=[x_two["up"]])
    forward_lift(0)
    third("down")
    land()
    forward_lower(0)
    forward_attend(1)
    forward_lift(1)
    forward_lower(1)

    pair = [((chips,) + block, BF16)] * 2
    keep, came, fanned, last = {}, {}, {}, {}
    sums = [{} for _ in range(layers)]
    flowing = [None] * (layers + 1)
    flowing[layers] = grad

    def leave(piece, send, kept_blocks):
        keep[piece] = kept_blocks
        came[piece] = core_flip(send)

    def back_lower(layer):
        s = kept[layer]
        s["sum_grad"], s["lowered_grad"], send, rest, sums[layer]["down"] = chain(
            functools.partial(lower_back, ordered=layer > 0),
            [row(F32), ((2, tall, width // 2), BF16)] + pair + [((8, width), F32)],
            smem=[tab], vmem=[flowing[layer + 1], s["unit_two"], s["scale_two"], vec[layer], s["activated"]],
        )
        leave((layer, "down"), send, rest)

    def back_lift(layer):
        s = kept[layer]
        s["lifted_grad"], send, rest, sums[layer]["up"] = chain(
            functools.partial(lift_back, ordered=layer > 0), [deep] + pair + [((8, width), F32)],
            smem=[tab], vmem=[s["lowered_grad"], s["slope"], s["middle"]], hbm=parts(layer, "down"),
            scratch=whole("down") + [pltpu.VMEM((width, tall), BF16)],
        )
        leave((layer, "up"), send, rest)

    def back_one(layer):
        s = kept[layer]
        s["first_grad"], s["attended_grad"], s["context_grad"], sums[layer]["one"] = chain(
            attend_back_first, [row(F32), ((2, tall, width // 2), BF16), row(BF16), ((8, width), F32)],
            smem=[tab], vmem=[s["sum_grad"], s["lifted_grad"], s["unit_one"], s["scale_one"], vec[layer]],
            hbm=parts(layer, "up") + parts(layer, "four"), scratch=whole("up") + whole("four", width // 2),
        )

    def back_two(layer):
        s = kept[layer]
        (s["grads"],) = chain(
            attend_back_second, [((2, tall, 2 * width), BF16)],
            vmem=[s["q"], s["k"], s["v"], s["p"], s["context_grad"], s["attended_grad"]],
        )

    def back_three(layer):
        s = kept[layer]
        send, rest, sums[layer]["four"] = chain(
            attend_back_third, pair + [((8, width), F32)], smem=[tab], vmem=[xs[layer], s["context"], s["grads"]],
            scratch=[pltpu.VMEM((width, tall), BF16)] * 2,
        )
        leave((layer, "four"), send, rest)

    def back_last(layer):
        s = kept[layer]
        (flowing[layer],) = chain(
            attend_back_last, [row(F32)], smem=[tab], vmem=[s["first_grad"], s["grads"]], hbm=parts(layer, "four"),
            scratch=whole("four", width * 3 // 2),
        )

    def fold(piece):
        half = keep[piece].shape[0] // 2
        send, keep[piece] = chain(add_halves, [((half,) + block, BF16)] * 2, vmem=[keep[piece], came[piece]])
        came[piece] = xy_two(send) if half == 2 * depth else xy_one(send)

    def fan(piece):
        made = chain(add_spread, [(block, F32)] + [(block, BF16)] * (depth - 1), vmem=[keep[piece], came[piece]])
        keep[piece] = made[0]
        fanned[piece] = [z_flip(made[k], k) for k in range(1, depth)]

    def owned(kind):
        return (block[0], block[1] // 2) if kind == "down" else (block[0] // 2, block[1])

    def total(pieces, values):
        outs = [(owned(kind), F32) for _, kind in pieces for _ in (0, 1)]
        made = chain(
            functools.partial(add_last, kinds=tuple(kind for _, kind in pieces)), outs, smem=[tab], vmem=values,
            scratch=[pltpu.VMEM((len(pieces) * block[0], block[1]), F32)],
        )
        for i, piece in enumerate(pieces):
            last[piece] = [made[2 * i], core_flip(made[2 * i + 1])]

    def finished(kind, count):
        height = down_weight.shape[1] if kind == "down" else rows
        columns = wide if kind == "up" else width
        return chain(
            functools.partial(write_out, kind=kind), [((layers, height, columns), F32)] * count, smem=[tab],
            vmem=[v for layer in range(layers) for v in last[layer, kind]],
        )

    back_lower(1)
    back_lift(1)
    d1, u1, f1, d0, u0, f0 = [(layer, kind) for layer in (1, 0) for kind in ("down", "up", "four")]
    back_one(1)
    (gone,) = chain(
        add_packed, [((chips, 2 * block[0], block[1]), BF16)], vmem=[keep[d1], came[d1], keep[u1], came[u1]]
    )
    gone = lax.psum_scatter(
        gone.reshape(-1, block[1]), "dp", scatter_dimension=0, tiled=True, axis_index_groups=same_core
    )
    back_two(1)
    back_three(1)
    back_last(1)
    fold(f1)
    back_lower(0)
    fold(f1)
    back_lift(0)
    fold(d0)
    fan(f1)
    back_one(0)
    fold(d0)
    fold(u0)
    total([f1], [keep[f1]] + fanned[f1])
    back_two(0)
    fan(d0)
    fold(u0)
    back_three(0)
    total([d0], [keep[d0]] + fanned[d0])
    total([d1, u1], [gone])
    fan(u0)
    fold(f0)
    rows_of = []
    for layer in range(layers):
        s = sums[layer]
        rows_of += [s["four"][0:2], s["one"][2:3], s["one"][0:2], s["down"][2:3], s["down"][0:2], s["up"][0 : wide // width]]
    vectors = jnp.concatenate(rows_of)
    back_last(0)
    fold(f0)
    total([u0], [keep[u0]] + fanned[u0])
    vector_round(0)
    vector_round(1)
    (down_grad,) = finished("down", 1)
    fan(f0)
    vector_round(2)
    (up_grad,) = finished("up", 1)
    vector_round(3)
    vector_round(4)
    total([f0], [keep[f0]] + fanned[f0])
    four_grads = finished("four", 4)

    order = [v for v in small if v.shape[1] == rows] + [v for v in small if v.shape[1] != rows]
    shares = own_share(vectors.reshape(layers, -1, width), [v.shape[1] for v in order], owners)
    cut = lambda values: values.reshape(items, ITEM, width)[:, :seq].reshape(items * seq, width)
    q_b, v_b, o_b, g_one, s_one, d_b, g_two, s_two, u_b = shares
    return (
        cut(xs[-1]), cut(flowing[0]), *four_grads,
        q_b, v_b, o_b, g_one, s_one, up_grad, u_b, down_grad, d_b, g_two, s_two,
    )


def shards(
    hidden, region_count, text_mask,
    q_weight, k_weight, v_weight, o_weight, q_bias, v_bias, o_bias, gain_one, shift_one,
    up_weight, up_bias, down_weight, down_bias, gain_two, shift_two, cotangent,
):
    owners = lax.axis_size("dp")
    valid_keys = slot_valid(region_count, text_mask)
    weights = (q_weight, k_weight, v_weight, o_weight, up_weight, down_weight)
    small = (q_bias, v_bias, o_bias, gain_one, shift_one, up_bias, down_bias, gain_two, shift_two)
    seq = valid_keys.shape[1]
    width = hidden.shape[1]
    fits = (
        owners in (16, 32)
        and q_weight.shape[1] % 8 == 0
        and up_weight.shape[2] % (2 * width) == 0
        and seq <= ITEM
        and q_weight.shape[0] == 2
    )
    if not fits:
        return plain(weights, small, valid_keys, hidden, cotangent)
    mask = (valid_keys - 1.0) * 10000.0
    mask = jnp.pad(mask, ((0, 0), (0, ITEM - seq)), constant_values=PAD)[:, None, :]
    return blocks(weights, small, mask, hidden, cotangent, seq)


def solution(mesh):
    rows = P("dp", None)
    matrix = P(None, "dp", None)
    vector = P(None, "dp")
    four = (matrix,) * 4
    return jax.shard_map(
        shards,
        mesh=mesh,
        in_specs=(rows, P("dp"), rows) + four + (vector,) * 5
        + (matrix, vector, matrix, vector, vector, vector, rows),
        out_specs=(rows, rows) + four + (vector,) * 5
        + (matrix, vector, matrix, vector, vector, vector),
        check_vma=False,
    )
```

time: 2470 us -> 553 us (0.22)
  Pallas kernels: 1770 us -> 192 us
  matrix products: 145 us -> 0.42 us
  waiting for transfers between devices: 267 us -> 180 us
  local copies, waits for them, and re-layouts: 137 us -> 71.3 us
  starting transfers between devices: 38.7 us -> 83.8 us
  other arithmetic: 44.3 us -> 0.24 us
  blocking collectives: 43.2 us -> 0 us
    pallas_call x24 -> x58, Pallas kernels: 1770 us -> 192 us  [launch(): pl.pallas_call(kernel, out_shape=[jax.ShapeDtypeStruct(s, d) for s, d in...]
    dot_general x46 -> x2, matrix products: 134 us -> 0.42 us  [spread(): return jnp.dot(values, hit.astype(BF16), preferred_element_type=F32)]
    ppermute x60 -> x70, waiting for transfers between devices: 267 us -> 169 us  [flip(): lax.ppermute(value, 'dp', [(i, i ^ (odd if i % 2 else even)) for i in ran...]
    ppermute x60 -> x70, starting transfers between devices: 38.6 us -> 83.7 us  [flip(): lax.ppermute(value, 'dp', [(i, i ^ (odd if i % 2 else even)) for i in ran...]
    all_gather x1 -> x0, blocking collectives: 43.2 us -> none  [shards(): packed = lax.all_gather(packed, 'dp', axis=0, tiled=True).astype(F32)]
    slice x65 -> x16, local copies, waits for them, and re-layouts: 45.2 us -> 2.2 us  [the longest x2 2.11 us: blocks(): values.reshape(items, ITEM, width)[:, :seq].reshape(items * seq, width)]
    unnamed x264 -> x226, local copies, waits for them, and re-layouts: 17.3 us -> 51.1 us
  transfers between devices with their start and end apart: 61 -> 72, of which waited for: 29 -> 26; matrix products, arithmetic and copies ran while one was open for 8% -> 4% of each run, Pallas kernels for 60% -> 24%
where the time goes in v2:
time: 553 us; the launch traced here: 543 us
  Pallas kernels  192 us (35%)
  waiting for transfers between devices  180 us (33%)
  starting transfers between devices  83.8 us (15%)
  local copies, waits for them, and re-layouts  71.3 us (13%)
  between operations  15.9 us (3%)
    pallas_call x58, Pallas kernels, launch(): pl.pallas_call(kernel, out_shape=[jax.ShapeDtypeStruct(s, d) for s, d in...  192 us
    ppermute x70, waiting for transfers between devices, flip(): lax.ppermute(value, 'dp', [(i, i ^ (odd if i % 2 else even)) for i in ran...  169 us
    ppermute x70, starting transfers between devices, flip(): lax.ppermute(value, 'dp', [(i, i ^ (odd if i % 2 else even)) for i in ran...  83.7 us
    unnamed x226, local copies, waits for them, and re-layouts  51.1 us
  transfers between devices with their start and end apart: 72, of which 26 were waited for; matrix products, arithmetic and copies ran while one was open for 4% of the time, Pallas kernels for 24%

profile of v2, /device:TPU:0, one launch (start us, length us, event | category | flops | bytes accessed | tf_op | source)
XLA Modules:
  0.0 543.2 jit_solution(5820613135143606143)
XLA Ops:
  29.1 10.6 %collective-permute-done.9.refs_2_ = bf16[48,1536]{1,0:T(8,128)(2,1)S(1)} collective-permute-done((bf16[48,1536]{1,0:T(8,128)(2,1)S(1)}, bf16[48,1536]{1,0:T(8,128)(2,1)S(1)}, u32[]{:S(2)}, u32[]{:S(2)}) %collective-permute-start.9) | collective-permute-done | bytes 147488 | tf_op jit(solution)/shard_map/ppermute | solution.py:218
  42.6 9.9 %collective-permute-done.7.refs_1_ = bf16[24,768]{1,0:T(8,128)(2,1)S(1)} collective-permute-done((bf16[24,768]{1,0:T(8,128)(2,1)S(1)}, bf16[24,768]{1,0:T(8,128)(2,1)S(1)}, u32[]{:S(2)}, u32[]{:S(2)}) %collective-permute-start.7) | collective-permute-done | bytes 36896 | tf_op jit(solution)/shard_map/ppermute | solution.py:218
  58.5 14.7 %collective-permute-start.12 = (bf16[24,768]{1,0:T(8,128)(2,1)S(1)}, bf16[24,768]{1,0:T(8,128)(2,1)S(1)}, u32[]{:S(2)}, u32[]{:S(2)}) collective-permute-start(bf16[24,768]{1,0:T(8,128)(2,1)S(1)} %add_two.12.refs_2_.refs_0_), channel_id=1, source_target_pairs={{0,8},{1,9},{2,10},{3,11},{4,12},{5,13},{6,14},{7,15},{8,0},{9,1},... | collective-permute-start | bytes 110600 | tf_op jit(solution)/shard_map/ppermute | solution.py:218
  78.8 7.3 %collective-permute-done.16.refs_2_ = bf16[48,1536]{1,0:T(8,128)(2,1)S(1)} collective-permute-done((bf16[48,1536]{1,0:T(8,128)(2,1)S(1)}, bf16[48,1536]{1,0:T(8,128)(2,1)S(1)}, u32[]{:S(2)}, u32[]{:S(2)}) %collective-permute-start.16) | collective-permute-done | bytes 147488 | tf_op jit(solution)/shard_map/ppermute | solution.py:218
  97.8 18.8 %collective-permute-done.24.refs_1_ = bf16[4,48,1536]{2,1,0:T(8,128)(2,1)S(1)} collective-permute-done((bf16[4,48,1536]{2,1,0:T(8,128)(2,1)S(1)}, bf16[4,48,1536]{2,1,0:T(8,128)(2,1)S(1)}, u32[]{:S(2)}, u32[]{:S(2)}) %collective-permute-start.24) | collective-permute-done | bytes 589856 | tf_op jit(solution)/shard_map/ppermute | solution.py:218
  130.3 16.5 %collective-permute-done.22.refs_2_ = bf16[192,384]{1,0:T(8,128)(2,1)S(1)} collective-permute-done((bf16[192,384]{1,0:T(8,128)(2,1)S(1)}, bf16[192,384]{1,0:T(8,128)(2,1)S(1)}, u32[]{:S(2)}, u32[]{:S(2)}) %collective-permute-start.22) | collective-permute-done | bytes 147488 | tf_op jit(solution)/shard_map/ppermute | solution.py:218
  150.2 14.5 %attend_forward.2 = (bf16[512,768]{1,0:T(8,128)(2,1)S(1)}, bf16[512,768]{1,0:T(8,128)(2,1)S(1)}, bf16[512,768]{1,0:T(8,128)(2,1)S(1)}, bf16[24,256,256]{2,1,0:T(...) custom-call(s32[65]{0:T(128)S(1)} %concatenate.13.refs_0_, ...), custom_call_target="tpu_custom_call" | custom-call | flops 17999998976 | bytes 54000000 | tf_op jit(solution)/shard_map/attend_forward/pallas_call | solution.py:252
  169.4 11.2 %lift.2 = (bf16[2,512,1536]{2,1,0:T(8,128)(2,1)S(1)}, bf16[2,512,1536]{2,1,0:T(8,128)(2,1)S(1)}) custom-call(s32[65]{0:T(128)S(1)} %concatenate.13.refs_0_, bf16[512,768]{1,0:T(8,128)(2,1)S(1)} %get-tuple-element.154.refs_1_.refs_2_.refs_3_, f32[12,768]{1,0:T(8,128)S(1)} %get-tuple-element.270.refs_2_.refs_3_.refs_4_.refs_5_, ...), custom_call_target="tpu_custom_call" | custom-call | flops 12999999488 | bytes 39000000 | tf_op jit(solution)/shard_map/lift/pallas_call | solution.py:252
  187.9 14.5 %collective-permute-done.29.refs_5_ = bf16[8,192,384]{2,1,0:T(8,128)(2,1)S(1)} collective-permute-done((bf16[8,192,384]{2,1,0:T(8,128)(2,1)S(1)}, bf16[8,192,384]{2,1,0:T(8,128)(2,1)S(1)}, u32[]{:S(2)}, u32[]{:S(2)}) %collective-permute-start.29) | collective-permute-done | bytes 1179680 | tf_op jit(solution)/shard_map/ppermute | solution.py:218
  208.4 7.9 %lower.2 = (bf16[512,768]{1,0:T(8,128)(2,1)S(1)}, f32[512,768]{1,0:T(8,128)S(1)}, f32[512,1]{1,0:T(8,128)S(1)}) custom-call(s32[65]{0:T(128)S(1)} %concatenate.13.refs_0_, bf16[2,512,1536]{2,1,0:T(8,128)(2,1)S(1)} %copy-done.62, bf16[512,768]{1,0:T(8,128)(2,1)S(1)} %copy-done.88, f32[12,768]{1,0:T(8,128)S(1)} %get-tuple-element.270.refs_2_.refs_3_.refs_4_.refs_5_, ...), custom_call_target="tpu_custom_call" | custom-call | flops 8999999488 | bytes 27000000 | tf_op jit(solution)/shard_map/lower/pallas_call | solution.py:252
  217.5 14.3 %attend_forward.3 = (bf16[512,768]{1,0:T(8,128)(2,1)S(1)}, bf16[512,768]{1,0:T(8,128)(2,1)S(1)}, bf16[512,768]{1,0:T(8,128)(2,1)S(1)}, bf16[24,256,256]{2,1,0:T(...) custom-call(s32[65]{0:T(128)S(1)} %concatenate.13.refs_0_, ...), custom_call_target="tpu_custom_call" | custom-call | flops 17999998976 | bytes 54000000 | tf_op jit(solution)/shard_map/attend_forward/pallas_call | solution.py:252
  232.7 11.7 %lift.3 = (bf16[2,512,1536]{2,1,0:T(8,128)(2,1)S(1)}, bf16[2,512,1536]{2,1,0:T(8,128)(2,1)S(1)}) custom-call(s32[65]{0:T(128)S(1)} %concatenate.13.refs_0_, bf16[512,768]{1,0:T(8,128)(2,1)S(1)} %get-tuple-element.160.refs_1_.refs_2_.refs_3_, f32[12,768]{1,0:T(8,128)S(1)} %get-tuple-element.269.refs_2_.refs_3_.refs_4_.refs_5_, ...), custom_call_target="tpu_custom_call" | custom-call | flops 12999999488 | bytes 39000000 | tf_op jit(solution)/shard_map/lift/pallas_call | solution.py:252
  244.4 8.0 %lower.3 = (bf16[512,768]{1,0:T(8,128)(2,1)S(1)}, f32[512,768]{1,0:T(8,128)S(1)}, f32[512,1]{1,0:T(8,128)S(1)}) custom-call(s32[65]{0:T(128)S(1)} %concatenate.13.refs_0_, bf16[2,512,1536]{2,1,0:T(8,128)(2,1)S(1)} %get-tuple-element.162.refs_1_.refs_6_.refs_5_, bf16[512,768]{1,0:T(8,128)(2,1)S(1)} %get-tuple-element.160.refs_1_.refs_2_.refs_3_, ...), custom_call_target="tpu_custom_call" | custom-call | flops 8999999488 | bytes 27000000 | tf_op jit(solution)/shard_map/lower/pallas_call | solution.py:252
  252.5 5.0 lower_back.2
  257.6 11.5 %lift_back.2 = (bf16[2,512,1536]{2,1,0:T(8,128)(2,1)S(1)}, bf16[16,48,1536]{2,1,0:T(8,128)(2,1)S(1)}, bf16[16,48,1536]{2,1,0:T(8,128)(2,1)S(1)}, f32[8,768]{1,0:T(8,128)S(1)}) custom-call(s32[65]{0:T(128)S(1)} %concatenate.13.refs_0_, bf16[2,512,384]{2,1,0:T(8,128)(2,1)S(1)} %get-tuple-element.167.refs_1_, ...), custom_call_target="tpu_custom_call" | custom-call | flops 15000000512 | bytes 45000000 | tf_op jit(solution)/shard_map/lift_back/pallas_call | solution.py:252
  269.6 10.9 %attend_back_first.2 = (f32[512,768]{1,0:T(8,128)S(1)}, bf16[2,512,384]{2,1,0:T(8,128)(2,1)S(1)}, bf16[512,768]{1,0:T(8,128)(2,1)S(1)}, f32[8,768]{1,0:T(8,128)S(1)}) custom-call(s32[65]{0:T(128)S(1)} %concatenate.13.refs_0_, f32[512,768]{1,0:T(8,128)S(1)} %get-tuple-element.166.refs_1_, bf16[2,512,1536]{2,1,0:T(8,128)(2,1)S(1)} %get-tuple-element.170.refs_2_, ...), custom_call_target="tpu_custom_call" | custom-call | flops 12999999488 | bytes 39000000 | tf_op jit(solution)/shard_map/attend_back_first/pallas_call | solution.py:252
  283.8 10.4 %attend_back_second.2.refs_3_.refs_4_.refs_2_ = bf16[2,512,1536]{2,1,0:T(8,128)(2,1)S(1)} custom-call(bf16[512,768]{1,0:T(8,128)(2,1)S(1)} %get-tuple-element.174.refs_0_, bf16[512,768]{1,0:T(8,128)(2,1)S(1)} %get-tuple-element.175.refs_1_, bf16[512,768]{1,0:T(8,128)(2,1)S(1)} %get-tuple-element.176.refs_2_, bf16[24,256,256]{2,1,0:T(8,128)(2,1)S(1)} %copy-done.71, ...), custom_call_target="tpu_custom_call" | custom-call | flops 10000000000 | bytes 30000000 | tf_op jit(solution)/shard_map/attend_back_second/pallas_call | solution.py:252
  306.2 5.6 %attend_back_last.2.refs_2_.refs_1_ = f32[512,768]{1,0:T(8,128)S(1)} custom-call(s32[65]{0:T(128)S(1)} %concatenate.13.refs_0_, f32[512,768]{1,0:T(8,128)S(1)} %copy-done.46, bf16[2,512,1536]{2,1,0:T(8,128)(2,1)S(1)} %copy-done.44, bf16[16,144,1536]{2,1,0:T(8,128)(2,1)S(1)} %bitcast.48, ...), custom_call_target="tpu_custom_call" | custom-call | flops 6000000000 | bytes 18000000 | tf_op jit(solution)/shard_map/attend_back_last/pallas_call | solution.py:252
  316.1 5.0 lower_back.3
  321.1 11.6 %collective-permute-done.36.refs_1_ = bf16[8,48,1536]{2,1,0:T(8,128)(2,1)S(1)} collective-permute-done((bf16[8,48,1536]{2,1,0:T(8,128)(2,1)S(1)}, bf16[8,48,1536]{2,1,0:T(8,128)(2,1)S(1)}, u32[]{:S(2)}, u32[]{:S(2)}) %collective-permute-start.36) | collective-permute-done | bytes 1179680 | tf_op jit(solution)/shard_map/ppermute | solution.py:218
  335.6 11.5 %lift_back.3 = (bf16[2,512,1536]{2,1,0:T(8,128)(2,1)S(1)}, bf16[16,48,1536]{2,1,0:T(8,128)(2,1)S(1)}, bf16[16,48,1536]{2,1,0:T(8,128)(2,1)S(1)}, f32[8,768]{1,0:T(8,128)S(1)}) custom-call(s32[65]{0:T(128)S(1)} %concatenate.13.refs_0_, bf16[2,512,384]{2,1,0:T(8,128)(2,1)S(1)} %get-tuple-element.192.refs_1_, bf16[2,512,1536]{2,1,0:T(8,128)(2,1)S(1)} %copy-done.86, ...), custom_call_target="tpu_custom_call" | custom-call | flops 15000000512 | bytes 45000000 | tf_op jit(solution)/shard_map/lift_back/pallas_call | solution.py:252
  350.0 15.8 %collective-permute-done.37.refs_1_ = bf16[4,48,1536]{2,1,0:T(8,128)(2,1)S(1)} collective-permute-done((bf16[4,48,1536]{2,1,0:T(8,128)(2,1)S(1)}, bf16[4,48,1536]{2,1,0:T(8,128)(2,1)S(1)}, u32[]{:S(2)}, u32[]{:S(2)}) %collective-permute-start.37) | collective-permute-done | bytes 589856 | tf_op jit(solution)/shard_map/ppermute | solution.py:218
  366.0 7.8 %collective-permute-start.39 = (bf16[48,1536]{1,0:T(8,128)(2,1)S(1)}, bf16[48,1536]{1,0:T(8,128)(2,1)S(1)}, u32[]{:S(2)}, u32[]{:S(2)}) collective-permute-start(bf16[48,1536]{1,0:T(8,128)(2,1)S(1)} %get-tuple-element.212), channel_id=1, source_target_pairs={{0,8},{1,9},{2,10},{3,11},{4,12},{5,13},{6,14},{7,15},{8,0},{9,1},... | collective-permute-start | bytes 442376 | tf_op jit(solution)/shard_map/ppermute | solution.py:218
  376.3 10.5 %attend_back_first.3 = (f32[512,768]{1,0:T(8,128)S(1)}, bf16[2,512,384]{2,1,0:T(8,128)(2,1)S(1)}, bf16[512,768]{1,0:T(8,128)(2,1)S(1)}, f32[8,768]{1,0:T(8,128)S(1)}) custom-call(s32[65]{0:T(128)S(1)} %concatenate.13.refs_0_, f32[512,768]{1,0:T(8,128)S(1)} %get-tuple-element.191.refs_1_, bf16[2,512,1536]{2,1,0:T(8,128)(2,1)S(1)} %get-tuple-element.197.refs_2_, ...), custom_call_target="tpu_custom_call" | custom-call | flops 12999999488 | bytes 39000000 | tf_op jit(solution)/shard_map/attend_back_first/pallas_call | solution.py:252
  389.2 5.0 collective-permute-start.44
  394.9 10.2 %attend_back_second.3.refs_2_.refs_3_ = bf16[2,512,1536]{2,1,0:T(8,128)(2,1)S(1)} custom-call(bf16[512,768]{1,0:T(8,128)(2,1)S(1)} %copy-done.95, bf16[512,768]{1,0:T(8,128)(2,1)S(1)} %copy-done.97, bf16[512,768]{1,0:T(8,128)(2,1)S(1)} %copy-done.99, bf16[24,256,256]{2,1,0:T(8,128)(2,1)S(1)} %copy-done.77, bf16[512,768]{1,0:T(8,128)(2,1)S(1)} %get-tuple-element.210.refs_4_, ...), custom_call_target="tpu_custom_call" | custom-call | flops 10000000000 | bytes 30000000 | tf_op jit(solution)/shard_map/attend_back_second/pallas_call | solution.py:252
  405.2 13.6 %collective-permute-done.44.refs_1_ = bf16[8,48,1536]{2,1,0:T(8,128)(2,1)S(1)} collective-permute-done((bf16[8,48,1536]{2,1,0:T(8,128)(2,1)S(1)}, bf16[8,48,1536]{2,1,0:T(8,128)(2,1)S(1)}, u32[]{:S(2)}, u32[]{:S(2)}) %collective-permute-start.44) | collective-permute-done | bytes 1179680 | tf_op jit(solution)/shard_map/ppermute | solution.py:218
  433.5 5.8 %collective-permute-done.50.refs_4_ = bf16[48,1536]{1,0:T(8,128)(2,1)S(1)} collective-permute-done((bf16[48,1536]{1,0:T(8,128)(2,1)S(1)}, bf16[48,1536]{1,0:T(8,128)(2,1)S(1)}, u32[]{:S(2)}, u32[]{:S(2)}) %collective-permute-start.50) | collective-permute-done | bytes 147488 | tf_op jit(solution)/shard_map/ppermute | solution.py:218
  441.3 10.6 %reduce-scatter.2.cloned.1.call-done.refs_1_ = bf16[96,1536]{1,0:T(8,128)(2,1)} async-done(((bf16[1536,1536]{1,0:T(8,128)(2,1)}), bf16[96,1536]{1,0:T(8,128)(2,1)}) %reduce-scatter.2.cloned.1.call-update) | async-done | bytes 294928 | tf_op jit(solution)/shard_map/reduce_scatter | solution.py:1011
  476.3 5.9 %attend_back_last.3.refs_2_ = f32[512,768]{1,0:T(8,128)S(1)} custom-call(s32[65]{0:T(128)S(1)} %concatenate.13.refs_0_, f32[512,768]{1,0:T(8,128)S(1)} %copy-done.60, bf16[2,512,1536]{2,1,0:T(8,128)(2,1)S(1)} %copy-done.50, bf16[8,48,1536]{2,1,0:T(8,128)(2,1)S(1)} %copy-done.8, bf16[8,48,1536]{2,1,0:T(8,128)(2,1)S(1)} %copy-done.11, ...), custom_call_target="tpu_custom_call" | custom-call | flops 6000000000 | bytes 18000000 | tf_op jit(solution)/shard_map/attend_back_last/pallas_call | solution.py:252
  487.3 7.5 %collective-permute-done.59.refs_1_ = f32[24,768]{1,0:T(8,128)S(1)} collective-permute-done((f32[24,768]{1,0:T(8,128)S(1)}, f32[24,768]{1,0:T(8,128)S(1)}, u32[]{:S(2)}, u32[]{:S(2)}) %collective-permute-start.59) | collective-permute-done | bytes 73760 | tf_op jit(solution)/shard_map/ppermute | solution.py:218
  521.3 6.8 %collective-permute-done.61.refs_3_ = bf16[48,1536]{1,0:T(8,128)(2,1)S(1)} collective-permute-done((bf16[48,1536]{1,0:T(8,128)(2,1)S(1)}, bf16[48,1536]{1,0:T(8,128)(2,1)S(1)}, u32[]{:S(2)}, u32[]{:S(2)}) %collective-permute-start.61) | collective-permute-done | bytes 147488 | tf_op jit(solution)/shard_map/ppermute | solution.py:218
  (457 shorter events, 195.9 us)
Async XLA Ops:
  7.2 178.8 %all-gather.2.cloned.1.call-start = ((), (), s32[]{:S(2)}) async-start(), calls=%async_computation.1 | async-start | bytes 7520256 | tf_op jit(solution)/shard_map/all_gather | solution.py:827
  16.9 435.0 %reduce-scatter.2.cloned.1.call-start = ((), (), s32[]{:S(2)}) async-start(), calls=%async_computation.2 | async-start | bytes 5013504 | tf_op jit(solution)/shard_map/reduce_scatter | solution.py:1011
  22.6 17.2 %collective-permute-start.9 = (bf16[48,1536]{1,0:T(8,128)(2,1)S(1)}, bf16[48,1536]{1,0:T(8,128)(2,1)S(1)}, u32[]{:S(2)}, u32[]{:S(2)}) collective-permute-start(bf16[48,1536]{1,0:T(8,128)(2,1)S(1)} %get-tuple-element.151.refs_2_.refs_0_), channel_id=1, source_target_pairs={{0,16},{1,17},{2,18},{3,19},{4,20},{5,21},{6,22},{7,23},{8,24},{9,... | collective-permute-start | bytes 442376 | tf_op jit(solution)/shard_map/ppermute | solution.py:218
  57.4 59.2 %collective-permute-start.18 = (bf16[8,48,1536]{2,1,0:T(8,128)(2,1)S(1)}, bf16[8,48,1536]{2,1,0:T(8,128)(2,1)S(1)}, u32[]{:S(2)}, u32[]{:S(2)}) collective-permute-start(bf16[8,48,1536]{2,1,0:T(8,128)(2,1)S(1)} %join_blocks.7.refs_2_.refs_4_.refs_10_.refs_3_), channel_id=1, source_target_pairs={{0,4},{1,3},{2,6},{3,1},{4,0},{5,7},{6,2},{7,5},{8,12},{9,11},{10,... | collective-permute-start | bytes 3538952 | tf_op jit(solution)/shard_map/ppermute | solution.py:218
  58.5 19.1 %collective-permute-start.12 = (bf16[24,768]{1,0:T(8,128)(2,1)S(1)}, bf16[24,768]{1,0:T(8,128)(2,1)S(1)}, u32[]{:S(2)}, u32[]{:S(2)}) collective-permute-start(bf16[24,768]{1,0:T(8,128)(2,1)S(1)} %add_two.12.refs_2_.refs_0_), channel_id=1, source_target_pairs={{0,8},{1,9},{2,10},{3,11},{4,12},{5,13},{6,14},{7,15},{8,0},{9,1},... | collective-permute-start | bytes 110600 | tf_op jit(solution)/shard_map/ppermute | solution.py:218
  91.0 25.6 %collective-permute-start.24 = (bf16[4,48,1536]{2,1,0:T(8,128)(2,1)S(1)}, bf16[4,48,1536]{2,1,0:T(8,128)(2,1)S(1)}, u32[]{:S(2)}, u32[]{:S(2)}) collective-permute-start(bf16[4,48,1536]{2,1,0:T(8,128)(2,1)S(1)} %join_blocks.8.refs_2_.refs_0_), channel_id=1, source_target_pairs={{0,2},{1,5},{2,0},{3,7},{4,6},{5,1},{6,4},{7,3},{8,10},{9,13},{10,... | collective-permute-start | bytes 1769480 | tf_op jit(solution)/shard_map/ppermute | solution.py:218
  118.0 31.8 %collective-permute-start.25 = (bf16[8,48,1536]{2,1,0:T(8,128)(2,1)}, bf16[8,48,1536]{2,1,0:T(8,128)(2,1)}, u32[]{:S(2)}, u32[]{:S(2)}) collective-permute-start(bf16[8,48,1536]{2,1,0:T(8,128)(2,1)} %join_blocks.9.refs_4_.refs_3_.refs_6_), channel_id=1, source_target_pairs={{0,4},{1,3},{2,6},{3,1},{4,0},{5,7},{6,2},{7,5},{8,12},{9,11},{10,... | collective-permute-start | bytes 3538952 | tf_op jit(solution)/shard_map/ppermute | solution.py:218
  119.0 31.2 %collective-permute-start.19 = (bf16[8,48,1536]{2,1,0:T(8,128)(2,1)S(1)}, bf16[8,48,1536]{2,1,0:T(8,128)(2,1)}, u32[]{:S(2)}, u32[]{:S(2)}) collective-permute-start(bf16[8,48,1536]{2,1,0:T(8,128)(2,1)S(1)} %join_blocks.7.refs_2_.refs_4_.refs_10_.refs_3_), channel_id=1, source_target_pairs={{0,1},{1,0},{2,3},{3,2},{4,5},{5,4},{6,7},{7,6},{8,9},{9,8},{10,11... | collective-permute-start | bytes 3538952 | tf_op jit(solution)/shard_map/ppermute | solution.py:218
  119.0 31.2 %collective-permute-start.20 = (bf16[8,48,1536]{2,1,0:T(8,128)(2,1)S(1)}, bf16[8,48,1536]{2,1,0:T(8,128)(2,1)}, u32[]{:S(2)}, u32[]{:S(2)}) collective-permute-start(bf16[8,48,1536]{2,1,0:T(8,128)(2,1)S(1)} %collective-permute-done.18.refs_2_.refs_5_.refs_11_.refs_4_), channel_id=1, source_target_pairs={{0,1},{1,0},{2,3},{3,2},{4,5},{5,4},{6,7},{7,6},{8,9},{9,8},{10,11... | collective-permute-start | bytes 3538952 | tf_op jit(solution)/shard_map/ppermute | solution.py:218
  125.9 20.9 %collective-permute-start.22 = (bf16[192,384]{1,0:T(8,128)(2,1)S(1)}, bf16[192,384]{1,0:T(8,128)(2,1)S(1)}, u32[]{:S(2)}, u32[]{:S(2)}) collective-permute-start(bf16[192,384]{1,0:T(8,128)(2,1)S(1)} %get-tuple-element.153.refs_0_), channel_id=1, source_target_pairs={{0,16},{1,17},{2,18},{3,19},{4,20},{5,21},{6,22},{7,23},{8,24},{9,... | collective-permute-start | bytes 442376 | tf_op jit(solution)/shard_map/ppermute | solution.py:218
  146.8 22.4 %collective-permute-start.26 = (bf16[8,48,1536]{2,1,0:T(8,128)(2,1)}, bf16[8,48,1536]{2,1,0:T(8,128)(2,1)S(1)}, u32[]{:S(2)}, u32[]{:S(2)}) collective-permute-start(bf16[8,48,1536]{2,1,0:T(8,128)(2,1)} %join_blocks.9.refs_4_.refs_3_.refs_6_), channel_id=1, source_target_pairs={{0,1},{1,0},{2,3},{3,2},{4,5},{5,4},{6,7},{7,6},{8,9},{9,8},{10,11... | collective-permute-start | bytes 3538952 | tf_op jit(solution)/shard_map/ppermute | solution.py:218
  147.9 18.6 %collective-permute-start.28 = (bf16[4,192,384]{2,1,0:T(8,128)(2,1)S(1)}, bf16[4,192,384]{2,1,0:T(8,128)(2,1)S(1)}, u32[]{:S(2)}, u32[]{:S(2)}) collective-permute-start(bf16[4,192,384]{2,1,0:T(8,128)(2,1)S(1)} %join_blocks.10.refs_8_.refs_0_), channel_id=1, source_target_pairs={{0,2},{1,5},{2,0},{3,7},{4,6},{5,1},{6,4},{7,3},{8,10},{9,13},{10,... | collective-permute-start | bytes 1769480 | tf_op jit(solution)/shard_map/ppermute | solution.py:218
  149.8 19.5 %collective-permute-start.27 = (bf16[8,48,1536]{2,1,0:T(8,128)(2,1)}, bf16[8,48,1536]{2,1,0:T(8,128)(2,1)S(1)}, u32[]{:S(2)}, u32[]{:S(2)}) collective-permute-start(bf16[8,48,1536]{2,1,0:T(8,128)(2,1)} %collective-permute-done.25.refs_2_.refs_4_.refs_7_), channel_id=1, source_target_pairs={{0,1},{1,0},{2,3},{3,2},{4,5},{5,4},{6,7},{7,6},{8,9},{9,8},{10,11... | collective-permute-start | bytes 3538952 | tf_op jit(solution)/shard_map/ppermute | solution.py:218
  186.0 31.4 %collective-permute-start.32 = (bf16[16,144,1536]{2,1,0:T(8,128)(2,1)}, bf16[16,144,1536]{2,1,0:T(8,128)(2,1)}, u32[]{:S(2)}, u32[]{:S(2)}) collective-permute-start(bf16[16,144,1536]{2,1,0:T(8,128)(2,1)} %bitcast.39), channel_id=1, source_target_pairs={{0,1},{1,0},{2,3},{3,2},{4,5},{5,4},{6,7},{7,6},{8,9},{9,8},{10,11... | collective-permute-start | bytes 21233672 | tf_op jit(solution)/shard_map/ppermute | solution.py:218
  187.9 18.4 %collective-permute-start.30 = (bf16[8,192,384]{2,1,0:T(8,128)(2,1)S(1)}, bf16[8,192,384]{2,1,0:T(8,128)(2,1)}, u32[]{:S(2)}, u32[]{:S(2)}) collective-permute-start(bf16[8,192,384]{2,1,0:T(8,128)(2,1)S(1)} %join_blocks.11.refs_7_.refs_4_), channel_id=1, source_target_pairs={{0,1},{1,0},{2,3},{3,2},{4,5},{5,4},{6,7},{7,6},{8,9},{9,8},{10,11... | collective-permute-start | bytes 3538952 | tf_op jit(solution)/shard_map/ppermute | solution.py:218
  257.5 23.1 %collective-permute-start.33 = (bf16[16,48,1536]{2,1,0:T(8,128)(2,1)S(1)}, bf16[16,48,1536]{2,1,0:T(8,128)(2,1)S(1)}, u32[]{:S(2)}, u32[]{:S(2)}) collective-permute-start(bf16[16,48,1536]{2,1,0:T(8,128)(2,1)S(1)} %get-tuple-element.181), channel_id=1, source_target_pairs={{0,1},{1,0},{2,3},{3,2},{4,5},{5,4},{6,7},{7,6},{8,9},{9,8},{10,11... | collective-permute-start | bytes 7077896 | tf_op jit(solution)/shard_map/ppermute | solution.py:218
  314.4 18.4 %collective-permute-start.36 = (bf16[8,48,1536]{2,1,0:T(8,128)(2,1)S(1)}, bf16[8,48,1536]{2,1,0:T(8,128)(2,1)S(1)}, u32[]{:S(2)}, u32[]{:S(2)}) collective-permute-start(bf16[8,48,1536]{2,1,0:T(8,128)(2,1)S(1)} %get-tuple-element.190.refs_6_), channel_id=1, source_target_pairs={{0,4},{1,3},{2,6},{3,1},{4,0},{5,7},{6,2},{7,5},{8,12},{9,11},{10,... | collective-permute-start | bytes 3538952 | tf_op jit(solution)/shard_map/ppermute | solution.py:218
  321.0 27.5 %collective-permute-start.38 = (bf16[16,48,1536]{2,1,0:T(8,128)(2,1)S(1)}, bf16[16,48,1536]{2,1,0:T(8,128)(2,1)S(1)}, u32[]{:S(2)}, u32[]{:S(2)}) collective-permute-start(bf16[16,48,1536]{2,1,0:T(8,128)(2,1)S(1)} %get-tuple-element.201), channel_id=1, source_target_pairs={{0,1},{1,0},{2,3},{3,2},{4,5},{5,4},{6,7},{7,6},{8,9},{9,8},{10,11... | collective-permute-start | bytes 7077896 | tf_op jit(solution)/shard_map/ppermute | solution.py:218
  347.1 41.4 %collective-permute-start.42 = (bf16[16,48,1536]{2,1,0:T(8,128)(2,1)S(1)}, bf16[16,48,1536]{2,1,0:T(8,128)(2,1)S(1)}, u32[]{:S(2)}, u32[]{:S(2)}) collective-permute-start(bf16[16,48,1536]{2,1,0:T(8,128)(2,1)S(1)} %get-tuple-element.216), channel_id=1, source_target_pairs={{0,1},{1,0},{2,3},{3,2},{4,5},{5,4},{6,7},{7,6},{8,9},{9,8},{10,11... | collective-permute-start | bytes 7077896 | tf_op jit(solution)/shard_map/ppermute | solution.py:218
  347.2 18.7 %collective-permute-start.37 = (bf16[4,48,1536]{2,1,0:T(8,128)(2,1)S(1)}, bf16[4,48,1536]{2,1,0:T(8,128)(2,1)S(1)}, u32[]{:S(2)}, u32[]{:S(2)}) collective-permute-start(bf16[4,48,1536]{2,1,0:T(8,128)(2,1)S(1)} %get-tuple-element.196.refs_8_), channel_id=1, source_target_pairs={{0,2},{1,5},{2,0},{3,7},{4,6},{5,1},{6,4},{7,3},{8,10},{9,13},{10,... | collective-permute-start | bytes 1769480 | tf_op jit(solution)/shard_map/ppermute | solution.py:218
  349.1 38.9 %collective-permute-start.43 = (bf16[8,48,1536]{2,1,0:T(8,128)(2,1)S(1)}, bf16[8,48,1536]{2,1,0:T(8,128)(2,1)S(1)}, u32[]{:S(2)}, u32[]{:S(2)}) collective-permute-start(bf16[8,48,1536]{2,1,0:T(8,128)(2,1)S(1)} %get-tuple-element.203.refs_2_), channel_id=1, source_target_pairs={{0,4},{1,3},{2,6},{3,1},{4,0},{5,7},{6,2},{7,5},{8,12},{9,11},{10,... | collective-permute-start | bytes 3538952 | tf_op jit(solution)/shard_map/ppermute | solution.py:218
  366.0 28.1 %collective-permute-start.39 = (bf16[48,1536]{1,0:T(8,128)(2,1)S(1)}, bf16[48,1536]{1,0:T(8,128)(2,1)S(1)}, u32[]{:S(2)}, u32[]{:S(2)}) collective-permute-start(bf16[48,1536]{1,0:T(8,128)(2,1)S(1)} %get-tuple-element.212), channel_id=1, source_target_pairs={{0,8},{1,9},{2,10},{3,11},{4,12},{5,13},{6,14},{7,15},{8,0},{9,1},... | collective-permute-start | bytes 442376 | tf_op jit(solution)/shard_map/ppermute | solution.py:218
  373.8 20.3 %collective-permute-start.40 = (bf16[48,1536]{1,0:T(8,128)(2,1)S(1)}, bf16[48,1536]{1,0:T(8,128)(2,1)S(1)}, u32[]{:S(2)}, u32[]{:S(2)}) collective-permute-start(bf16[48,1536]{1,0:T(8,128)(2,1)S(1)} %get-tuple-element.213), channel_id=1, source_target_pairs={{0,16},{1,17},{2,18},{3,19},{4,20},{5,21},{6,22},{7,23},{8,24},{9,... | collective-permute-start | bytes 442376 | tf_op jit(solution)/shard_map/ppermute | solution.py:218
  373.8 20.3 %collective-permute-start.41 = (bf16[48,1536]{1,0:T(8,128)(2,1)S(1)}, bf16[48,1536]{1,0:T(8,128)(2,1)S(1)}, u32[]{:S(2)}, u32[]{:S(2)}) collective-permute-start(bf16[48,1536]{1,0:T(8,128)(2,1)S(1)} %get-tuple-element.214), channel_id=1, source_target_pairs={{0,24},{1,25},{2,26},{3,27},{4,28},{5,29},{6,30},{7,31},{8,16},{9,... | collective-permute-start | bytes 442376 | tf_op jit(solution)/shard_map/ppermute | solution.py:218
  389.2 29.7 %collective-permute-start.44 = (bf16[8,48,1536]{2,1,0:T(8,128)(2,1)S(1)}, bf16[8,48,1536]{2,1,0:T(8,128)(2,1)S(1)}, u32[]{:S(2)}, u32[]{:S(2)}) collective-permute-start(bf16[8,48,1536]{2,1,0:T(8,128)(2,1)S(1)} %get-tuple-element.220.refs_5_), channel_id=1, source_target_pairs={{0,4},{1,3},{2,6},{3,1},{4,0},{5,7},{6,2},{7,5},{8,12},{9,11},{10,... | collective-permute-start | bytes 3538952 | tf_op jit(solution)/shard_map/ppermute | solution.py:218
  426.1 33.2 %collective-permute-start.46 = (bf16[16,48,1536]{2,1,0:T(8,128)(2,1)S(1)}, bf16[16,48,1536]{2,1,0:T(8,128)(2,1)}, u32[]{:S(2)}, u32[]{:S(2)}) collective-permute-start(bf16[16,48,1536]{2,1,0:T(8,128)(2,1)S(1)} %get-tuple-element.228), channel_id=1, source_target_pairs={{0,1},{1,0},{2,3},{3,2},{4,5},{5,4},{6,7},{7,6},{8,9},{9,8},{10,11... | collective-permute-start | bytes 7077896 | tf_op jit(solution)/shard_map/ppermute | solution.py:218
  426.1 29.7 %collective-permute-start.47 = (bf16[4,48,1536]{2,1,0:T(8,128)(2,1)}, bf16[4,48,1536]{2,1,0:T(8,128)(2,1)}, u32[]{:S(2)}, u32[]{:S(2)}) collective-permute-start(bf16[4,48,1536]{2,1,0:T(8,128)(2,1)} %get-tuple-element.226.refs_4_), channel_id=1, source_target_pairs={{0,2},{1,5},{2,0},{3,7},{4,6},{5,1},{6,4},{7,3},{8,10},{9,13},{10,... | collective-permute-start | bytes 1769480 | tf_op jit(solution)/shard_map/ppermute | solution.py:218
  463.7 18.5 %collective-permute-start.51 = (bf16[8,48,1536]{2,1,0:T(8,128)(2,1)}, bf16[8,48,1536]{2,1,0:T(8,128)(2,1)}, u32[]{:S(2)}, u32[]{:S(2)}) collective-permute-start(bf16[8,48,1536]{2,1,0:T(8,128)(2,1)} %get-tuple-element.237.refs_7_), channel_id=1, source_target_pairs={{0,4},{1,3},{2,6},{3,1},{4,0},{5,7},{6,2},{7,5},{8,12},{9,11},{10,... | collective-permute-start | bytes 3538952 | tf_op jit(solution)/shard_map/ppermute | solution.py:218
  465.9 18.8 %collective-permute-start.55 = (f32[24,768]{1,0:T(8,128)S(1)}, f32[24,768]{1,0:T(8,128)S(1)}, u32[]{:S(2)}, u32[]{:S(2)}) collective-permute-start(f32[24,768]{1,0:T(8,128)S(1)} %concatenate.16.refs_0_), channel_id=1, source_target_pairs={{0,1},{1,0},{2,3},{3,2},{4,5},{5,4},{6,7},{7,6},{8,9},{9,8},{10,11... | collective-permute-start | bytes 221192 | tf_op jit(solution)/shard_map/ppermute | solution.py:218
  466.0 18.0 %collective-permute-start.56 = (bf16[48,1536]{1,0:T(8,128)(2,1)S(1)}, bf16[48,1536]{1,0:T(8,128)(2,1)S(1)}, u32[]{:S(2)}, u32[]{:S(2)}) collective-permute-start(bf16[48,1536]{1,0:T(8,128)(2,1)S(1)} %copy-done.34), channel_id=1, source_target_pairs={{0,8},{1,9},{2,10},{3,11},{4,12},{5,13},{6,14},{7,15},{8,0},{9,1},... | collective-permute-start | bytes 442376 | tf_op jit(solution)/shard_map/ppermute | solution.py:218
  466.0 17.9 %collective-permute-start.57 = (bf16[48,1536]{1,0:T(8,128)(2,1)S(1)}, bf16[48,1536]{1,0:T(8,128)(2,1)S(1)}, u32[]{:S(2)}, u32[]{:S(2)}) collective-permute-start(bf16[48,1536]{1,0:T(8,128)(2,1)S(1)} %copy-done.32), channel_id=1, source_target_pairs={{0,16},{1,17},{2,18},{3,19},{4,20},{5,21},{6,22},{7,23},{8,24},{9,... | collective-permute-start | bytes 442376 | tf_op jit(solution)/shard_map/ppermute | solution.py:218
  508.4 26.2 %collective-permute-start.69 = (f32[24,1536]{1,0:T(8,128)S(1)}, f32[24,1536]{1,0:T(8,128)S(1)}, u32[]{:S(2)}, u32[]{:S(2)}) collective-permute-start(f32[24,1536]{1,0:T(8,128)S(1)} %get-tuple-element.256), channel_id=1, source_target_pairs={{0,1},{1,0},{2,3},{3,2},{4,5},{5,4},{6,7},{7,6},{8,9},{9,8},{10,11... | collective-permute-start | bytes 442376 | tf_op jit(solution)/shard_map/ppermute | solution.py:218
  (152 other events, 1028.2 us)
Sparse Core Ops, SparseCore 0:
  17.0 141.1 all-gather.1
  300.0 151.9 reduce-scatter.1
